TPU v7x, 512 devices: a whole 4x8x8 slice. The times are simulated.
512 devices in a mesh: lat: 16 (over x_lo, z), lon: 32 (over x_hi, y, core).
Axes of the slice: x: 4 (x_hi: 2, x_lo: 2; x = x_hi * 2 + x_lo), y: 8, z: 8, core: 2. Of those that a mesh axis runs over, the one named last changes fastest.
Arguments:
- query_field: bfloat16 [1, 256, 512, 512], P(None, 'lat', 'lon'), may hold values from -6 to 6
- key_field: bfloat16 [1, 256, 512, 512], P(None, 'lat', 'lon'), may hold values from -6 to 6
- value_field: bfloat16 [1, 256, 512, 512], P(None, 'lat', 'lon'), may hold values from -6 to 6
- out_grad: bfloat16 [1, 256, 512, 1024], P(None, 'lat', 'lon'), may hold values from -6 to 6
- out_weight: bfloat16 [512, 1024], P('lat', 'lon'), may hold values from -0.25 to 0.25
- time_weight: bfloat16 [256, 1024], replicated, may hold values from -0.375 to 0.375
- rel_bias: float32 [8, 49], replicated, may hold values from -4 to 4
- timesteps: int32 [1], replicated, may hold values from 0 to 999
Outputs:
- query_grad: bfloat16 [1, 256, 512, 512], P(None, 'lat', 'lon')
- key_grad: bfloat16 [1, 256, 512, 512], P(None, 'lat', 'lon')
- value_grad: bfloat16 [1, 256, 512, 512], P(None, 'lat', 'lon')
- out_weight_grad: float32 [512, 1024], P('lat', 'lon')
- time_weight_grad: float32 [256, 1024], P('lat', 'lon')
- bias_grad: float32 [8, 49], replicated
All inputs are finite; a program needn't handle non-finite values.
Results may differ from a plain program's by a relative error of at most 0.022.
Values may be sent and summed in bfloat16 or wider, within the bound.
A program may use at most 128 MiB of HBM per device.

v0:
```python
import math

import jax
import jax.numpy as jnp
from jax import lax
from jax.sharding import PartitionSpec as P

SHIFT = 2


def extended(block, sides, width):
    for axis, dim in sides:
        count = lax.axis_size(axis)
        forward = [(i, i + 1) for i in range(count - 1)]
        forward.append((count - 1, 0))
        backward = [(target, source) for source, target in forward]
        low = lax.ppermute(
            lax.slice_in_dim(block, block.shape[dim] - width, None, axis=dim), axis, forward
        )
        high = lax.ppermute(lax.slice_in_dim(block, 0, width, axis=dim), axis, backward)
        block = jnp.concatenate([low, block, high], axis=dim)
    return block


def bucket_table():
    slots = jnp.arange(16, dtype=jnp.int32)
    row_gap = slots[:, None] // 4 - slots[None, :] // 4 + 3
    col_gap = slots[:, None] % 4 - slots[None, :] % 4 + 3
    index = (row_gap * 7 + col_gap).reshape(256)
    return (index[:, None] == jnp.arange(49, dtype=jnp.int32)[None, :]).astype(jnp.float32)


def time_embed(timesteps, width):
    half = width // 2
    freqs = jnp.exp(-math.log(10000.0) * jnp.arange(half, dtype=jnp.float32) / half)
    angles = timesteps.astype(jnp.float32)[:, None] * freqs[None, :]
    return jnp.concatenate([jnp.cos(angles), jnp.sin(angles)], axis=1)


def to_windows(field, heads):
    rows, cols, width = field.shape
    shaped = field.reshape(rows // 4, 4, cols // 4, 4, heads, width // heads)
    return shaped.transpose(0, 2, 1, 3, 4, 5).reshape(-1, 16, heads, width // heads)


def mask_windows(flags):
    rows, cols = flags.shape
    return flags.reshape(rows // 4, 4, cols // 4, 4).transpose(0, 2, 1, 3).reshape(-1, 16)


def from_windows(windows, rows, cols):
    heads, depth = (windows.shape[2], windows.shape[3])
    shaped = windows.reshape(rows // 4, cols // 4, 4, 4, heads, depth)
    return shaped.transpose(0, 2, 1, 3, 4, 5).reshape(rows, cols, heads * depth)


def window_pass(query_win, key_win, value_win, cot_win, key_ok, bias_full, scale):
    f32 = jnp.float32
    scores = (
        jnp.einsum("wqhd,wkhd->whqk", query_win, key_win, preferred_element_type=f32) * scale
        + bias_full[None]
    )
    scores = jnp.where(key_ok[:, None, None, :], scores, -1000000000.0)
    top = jnp.max(scores, axis=-1, keepdims=True)
    expo = jnp.exp(scores - top)
    probs = expo / jnp.sum(expo, axis=-1, keepdims=True)
    probs_b = probs.astype(jnp.bfloat16)
    attn = jnp.einsum("whqk,wkhd->wqhd", probs_b, value_win, preferred_element_type=f32).astype(
        jnp.bfloat16
    )
    dvalue = jnp.einsum("whqk,wqhd->wkhd", probs_b, cot_win, preferred_element_type=f32).astype(
        jnp.bfloat16
    )
    dprob = jnp.einsum("wqhd,wkhd->whqk", cot_win, value_win, preferred_element_type=f32)
    dscore = probs * (dprob - jnp.sum(probs * dprob, axis=-1, keepdims=True))
    dscore_b = dscore.astype(jnp.bfloat16)
    dquery = (
        jnp.einsum("whqk,wkhd->wqhd", dscore_b, key_win, preferred_element_type=f32) * scale
    ).astype(jnp.bfloat16)
    dkey = (
        jnp.einsum("whqk,wqhd->wkhd", dscore_b, query_win, preferred_element_type=f32) * scale
    ).astype(jnp.bfloat16)
    return (attn, dquery, dkey, dvalue, dscore)


def body(
    query_field, key_field, value_field, out_grad, out_weight, time_weight, rel_bias, timesteps
):
    f32 = jnp.float32
    high = lax.Precision.HIGHEST
    frames, tile_rows, tile_cols, width = query_field.shape
    model = out_grad.shape[3]
    heads = rel_bias.shape[0]
    lat_count = lax.axis_size("lat")
    lon_count = lax.axis_size("lon")
    lat_total = tile_rows * lat_count
    first_row = lax.axis_index("lat") * tile_rows
    factor = 1.0 / math.sqrt(frames * lat_total * tile_cols * lon_count)
    scale = (width // heads) ** (-0.5)
    emb = time_embed(timesteps, time_weight.shape[0])
    gate = jnp.dot(emb, time_weight.astype(f32), precision=high)
    table = bucket_table()
    bias_full = jnp.dot(rel_bias, table.T, precision=high).reshape(heads, 16, 16)
    row_band = lax.all_gather(out_weight, "lon", axis=1, tiled=True)
    full_weight = lax.all_gather(row_band, "lat", axis=0, tiled=True)
    gated_own = (out_grad.astype(f32) * gate[:, None, None, :]).astype(jnp.bfloat16)
    query_ext, key_ext, value_ext = (
        extended(query_field, (("lat", 1), ("lon", 2)), 2),
        extended(key_field, (("lat", 1), ("lon", 2)), 2),
        extended(value_field, (("lat", 1), ("lon", 2)), 2),
    )
    cot_ext = extended(
        lax.dot_general(
            gated_own, full_weight, (((3,), (1,)), ((), ())), preferred_element_type=f32
        ).astype(jnp.bfloat16),
        (("lat", 1), ("lon", 2)),
        2,
    )
    rows_region = tile_rows + 4
    cols_region = tile_cols + 4
    local_rows = jnp.arange(rows_region, dtype=jnp.int32)
    local_cols = jnp.arange(cols_region, dtype=jnp.int32)
    global_rows = first_row - SHIFT + local_rows
    valid = (global_rows >= 0) & (global_rows < lat_total)
    valid_grid = jnp.broadcast_to(valid[:, None], (rows_region, cols_region))
    owned_rows = (local_rows >= SHIFT) & (local_rows < SHIFT + tile_rows)
    owned_cols = (local_cols >= SHIFT) & (local_cols < SHIFT + tile_cols)
    owned = mask_windows(owned_rows[:, None] & owned_cols[None, :])
    key_ok = mask_windows(valid_grid)

    def back(windows):
        field = from_windows(windows, rows_region, cols_region)
        return field[SHIFT : SHIFT + tile_rows, SHIFT : SHIFT + tile_cols]

    query_list, key_list, value_list, gate_terms = ([], [], [], [])
    cot = jnp.where(valid[:, None, None], cot_ext[0], jnp.zeros((), jnp.bfloat16))
    attn_w, dq_w, dk_w, dv_w, dscore = window_pass(
        to_windows(query_ext[0], heads),
        to_windows(key_ext[0], heads),
        to_windows(value_ext[0], heads),
        to_windows(cot, heads),
        key_ok,
        bias_full,
        scale,
    )
    kept = jnp.sum(jnp.where(owned[:, None, :, None], dscore, 0.0), axis=0)
    bias_terms = jnp.dot(kept.reshape(heads, 256), table, precision=high)
    query_list.append(back(dq_w))
    key_list.append(back(dk_w))
    value_list.append(back(dv_w))
    attn = back(attn_w).reshape(-1, width)
    proj = jnp.dot(attn, full_weight, preferred_element_type=f32)
    gate_terms.append(jnp.sum(out_grad[0].astype(f32).reshape(-1, model) * proj, axis=0))
    weight_terms = jnp.dot(attn.T, gated_own[0].reshape(-1, model), preferred_element_type=f32)
    gate_part = jnp.stack(gate_terms, axis=0) * factor
    gate_sum, bias_grad = lax.psum((gate_part, bias_terms * factor), ("lat", "lon"))
    time_full = jnp.dot(emb.T, gate_sum, precision=high)
    emb_rows = time_full.shape[0] // lat_count
    model_cols = model // lon_count
    time_grad = lax.dynamic_slice(
        time_full,
        (lax.axis_index("lat") * emb_rows, lax.axis_index("lon") * model_cols),
        (emb_rows, model_cols),
    )
    weight_terms = weight_terms * factor
    column_band = lax.psum_scatter(weight_terms, "lon", scatter_dimension=1, tiled=True)
    weight_grad = lax.psum_scatter(
        column_band.astype(jnp.bfloat16), "lat", scatter_dimension=0, tiled=True
    ).astype(jnp.float32)
    return (
        jnp.stack(query_list, axis=0),
        jnp.stack(key_list, axis=0),
        jnp.stack(value_list, axis=0),
        weight_grad,
        time_grad,
        bias_grad,
    )


def solution(mesh):
    placed = (
        P(None, "lat", "lon", None),
        P(None, "lat", "lon", None),
        P(None, "lat", "lon", None),
        P(None, "lat", "lon", None),
        P("lat", "lon"),
        P(),
        P(),
        P(),
    )
    return jax.shard_map(
        body,
        mesh=mesh,
        in_specs=placed,
        out_specs=(
            P(None, "lat", "lon", None),
            P(None, "lat", "lon", None),
            P(None, "lat", "lon", None),
            P("lat", "lon"),
            P("lat", "lon"),
            P(),
        ),
        check_vma=False,
    )
```

profile of v0, /device:TPU:56, one launch (start us, length us, event | category | flops | bytes accessed | tf_op | source)
XLA Modules:
  0.0 358.7 jit_solution(11235040641435327273)
XLA Ops:
  8.1 0.9 fusion.25
  9.0 11.9 %collective-permute-start.5 = (bf16[1,2,16,512]{3,2,1,0:T(8,128)(2,1)S(1)}, bf16[1,2,16,512]{3,2,1,0:T(8,128)(2,1)S(1)}, u32[]{:S(2)}, u32[]{:S(2)}) collective-permute-start(bf16[1,2,16,512]{3,2,1,0:T(8,128)(2,1)S(1)} %get-tuple-element.42), channel_id=1, source_target_pairs={{32,0},{64,32},{96,64},{128,96},{160,128},{192,160},{224,192},{256... | collective-permute-start | bytes 98312 | tf_op jit(solution)/shard_map/ppermute | solution.py:20
  20.8 1.9 collective-permute-start.4
  22.8 0.8 fusion.28
  23.5 6.0 %collective-permute-start.1 = (bf16[1,2,16,512]{3,2,1,0:T(8,128)(2,1)S(1)}, bf16[1,2,16,512]{3,2,1,0:T(8,128)(2,1)S(1)}, u32[]{:S(2)}, u32[]{:S(2)}) collective-permute-start(bf16[1,2,16,512]{3,2,1,0:T(8,128)(2,1)S(1)} %get-tuple-element.48), channel_id=1, source_target_pairs={{32,0},{64,32},{96,64},{128,96},{160,128},{192,160},{224,192},{256... | collective-permute-start | bytes 98312 | tf_op jit(solution)/shard_map/ppermute | solution.py:20
  29.6 1.9 collective-permute-start
  31.5 0.8 fusion.26
  32.3 1.9 collective-permute-start.12
  34.2 0.8 copy.54
  35.0 36.4 %all_gather.6 = bf16[32,1024]{0,1:T(8,128)(2,1)S(1)} all-gather(bf16[32,32]{0,1:T(8,128)(2,1)S(1)} %copy.54), channel_id=1, replica_groups=mesh['lat'=16,'lon'=32] {'lon'}, dimensions={1}, use_global_device_ids=true | all-gather | bytes 67584 | tf_op jit(solution)/shard_map/all_gather | solution.py:104
  71.4 0.8 copy.55
  74.6 0.7 copy.53
  75.3 0.6 dynamic-slice
  75.9 6.0 %collective-permute-start.13 = (bf16[1,2,16,512]{3,2,1,0:T(8,128)(2,1)S(1)}, bf16[1,2,16,512]{3,2,1,0:T(8,128)(2,1)S(1)}, u32[]{:S(2)}, u32[]{:S(2)}) collective-permute-start(bf16[1,2,16,512]{3,2,1,0:T(8,128)(2,1)S(1)} %get-tuple-element.44), channel_id=1, source_target_pairs={{32,0},{64,32},{96,64},{128,96},{160,128},{192,160},{224,192},{256... | collective-permute-start | bytes 98312 | tf_op jit(solution)/shard_map/ppermute | solution.py:20
  81.9 1.5 collective-permute-done.13
  83.5 0.7 copy-done.8
  84.2 0.7 fusion.23
  84.9 1.9 collective-permute-start.14
  86.8 3.6 %collective-permute-start.15 = (bf16[1,20,2,512]{3,2,1,0:T(2,128)(2,1)}, bf16[1,20,2,512]{3,2,1,0:T(2,128)(2,1)}, u32[]{:S(2)}, u32[]{:S(2)}) collective-permute-start(bf16[1,20,2,512]{3,2,1,0:T(2,128)(2,1)} %get-tuple-element.37), channel_id=1, source_target_pairs={{1,0},{2,1},{3,2},{4,3},{5,4},{6,5},{7,6},{8,7},{9,8},{10,9},{11,1... | collective-permute-start | bytes 122888 | tf_op jit(solution)/shard_map/ppermute | solution.py:20
  90.6 7.1 %collective-permute-start.2 = (bf16[1,20,2,512]{3,2,1,0:T(2,128)(2,1)S(1)}, bf16[1,20,2,512]{3,2,1,0:T(2,128)(2,1)S(1)}, u32[]{:S(2)}, u32[]{:S(2)}) collective-permute-start(bf16[1,20,2,512]{3,2,1,0:T(2,128)(2,1)S(1)} %get-tuple-element.40), channel_id=1, source_target_pairs={{0,1},{1,2},{2,3},{3,4},{4,5},{5,6},{6,7},{7,8},{8,9},{9,10},{10,1... | collective-permute-start | bytes 122888 | tf_op jit(solution)/shard_map/ppermute | solution.py:17
  97.8 1.9 collective-permute-start.3
  99.9 7.3 %collective-permute-start.6 = (bf16[1,20,2,512]{3,2,1,0:T(2,128)(2,1)S(1)}, bf16[1,20,2,512]{3,2,1,0:T(2,128)(2,1)S(1)}, u32[]{:S(2)}, u32[]{:S(2)}) collective-permute-start(bf16[1,20,2,512]{3,2,1,0:T(2,128)(2,1)S(1)} %get-tuple-element.34), channel_id=1, source_target_pairs={{0,1},{1,2},{2,3},{3,4},{4,5},{5,6},{6,7},{7,8},{8,9},{9,10},{10,1... | collective-permute-start | bytes 122888 | tf_op jit(solution)/shard_map/ppermute | solution.py:17
  107.1 1.9 collective-permute-start.7
  109.1 1.0 pad_maximum_fusion
  110.1 5.0 %collective-permute-done.7 = bf16[1,20,2,512]{3,2,1,0:T(2,128)(2,1)S(1)} collective-permute-done((bf16[1,20,2,512]{3,2,1,0:T(2,128)(2,1)S(1)}, bf16[1,20,2,512]{3,2,1,0:T(2,128)(2,1)S(1)}, u32[]{:S(2)}, u32[]{:S(2)}) %collective-permute-start.7) | collective-permute-done | bytes 40992 | tf_op jit(solution)/shard_map/ppermute | solution.py:20
  115.4 0.4 reshape_squeeze.13
  116.2 1.6 reshape_squeeze.12
  118.3 0.5 copy-done.9
  118.8 1.8 pad_maximum_fusion.3
  120.6 1.6 reshape_squeeze.14
  122.2 1.4 copy.57
  123.6 3.7 %exponential_reduce_fusion = (f32[25,8,16]{2,1,0:T(8,128)}, f32[25,8,16,16]{2,3,1,0:T(8,128)}) fusion(bf16[25,16,8,64]{3,1,2,0:T(8,128)(2,1)S(1)} %bitcast.86, bf16[25,16,8,64]{3,1,2,0:T(8,128)(2,1)S(1)} %bitcast.88, f32[8,16,16]{1,2,0:T(8,128)} %copy.53, pred[25,16]{1,0:T(8,128)(4,1)S(1)} %broadcast_in_dim.34), kind=kOutput, calls=%fused_computation.10 | convolution fusion | flops 6809615 | bytes 1045392 | tf_op jit(solution)/shard_map/sub | solution.py:65
  127.3 2.0 convolution_convert_fusion.1
  129.6 1.3 reshape.328
  131.0 1.1 slice.91
  132.0 1.8 convolution_multiply_fusion
  134.0 10.4 %all-gather.2.cloned.1.call-done = bf16[512,1024]{1,0:T(8,128)(2,1)} async-done(((bf16[32,1024]{1,0:T(8,128)(2,1)}), bf16[512,1024]{1,0:T(8,128)(2,1)}) %all-gather.2.cloned.1.call-update) | async-done | bytes 1048592 | tf_op jit(solution)/shard_map/all_gather | solution.py:105
  144.3 1.8 fusion.3
  146.1 2.4 collective-permute-start.8
  148.6 5.5 %collective-permute-start.9 = (bf16[1,2,16,512]{3,2,1,0:T(8,128)(2,1)S(1)}, bf16[1,2,16,512]{3,2,1,0:T(8,128)(2,1)S(1)}, u32[]{:S(2)}, u32[]{:S(2)}) collective-permute-start(bf16[1,2,16,512]{3,2,1,0:T(8,128)(2,1)S(1)} %get-tuple-element.47), channel_id=1, source_target_pairs={{32,0},{64,32},{96,64},{128,96},{160,128},{192,160},{224,192},{256... | collective-permute-start | bytes 98312 | tf_op jit(solution)/shard_map/ppermute | solution.py:20
  154.1 0.4 fusion.2
  154.6 1.1 collective-permute-done.9
  155.7 1.9 collective-permute-start.10
  157.7 3.8 %collective-permute-start.11 = (bf16[1,20,2,512]{3,2,1,0:T(2,128)(2,1)S(1)}, bf16[1,20,2,512]{3,2,1,0:T(2,128)(2,1)S(1)}, u32[]{:S(2)}, u32[]{:S(2)}) collective-permute-start(bf16[1,20,2,512]{3,2,1,0:T(2,128)(2,1)S(1)} %get-tuple-element.39), channel_id=1, source_target_pairs={{1,0},{2,1},{3,2},{4,3},{5,4},{6,5},{7,6},{8,7},{9,8},{10,9},{11,1... | collective-permute-start | bytes 122888 | tf_op jit(solution)/shard_map/ppermute | solution.py:20
  161.5 1.5 collective-permute-done.11
  164.3 0.9 copy-done.1
  165.1 0.6 convolution_convert_fusion
  166.0 1.3 reshape.326
  167.4 2.8 multiply_reduce_fusion
  170.2 0.7 select_reduce_fusion
  171.0 0.4 multiply_convert_fusion.1
  171.8 1.4 reshape.322
  173.2 0.6 multiply_convert_fusion
  174.1 0.5 reshape.324
  174.9 102.6 %all-reduce = (f32[1024]{0:T(1024)S(1)}, f32[8,49]{1,0:T(8,128)}) all-reduce(f32[1024]{0:T(1024)S(1)} %broadcast_multiply_fusion.1, f32[8,49]{1,0:T(8,128)S(1)} %convolution_multiply_fusion.2), channel_id=1, replica_groups=mesh['lat'=16,'lon'=32] {'lat','lon'}, use_global_device_ids=true, to_apply=%region_6.7 | all-reduce | flops 1416 | bytes 11328 | tf_op jit(solution)/shard_map/psum | solution.py:156
  277.6 0.8 slice_bitcast_fusion
  278.4 0.8 slice_bitcast_fusion.2
  279.1 0.8 slice_bitcast_fusion.1
  279.9 0.8 convert_element_type.75
  280.8 0.8 copy.68
  281.6 0.7 broadcast_multiply_fusion
  282.2 67.6 %reduce-scatter.7.cloned.1.call-done = bf16[32,32]{1,0:T(8,128)(2,1)} async-done(((bf16[512,32]{1,0:T(8,128)(2,1)}), bf16[32,32]{1,0:T(8,128)(2,1)}) %reduce-scatter.7.cloned.1.call-update) | async-done | bytes 2064
  349.8 0.8 copy.69
  350.6 0.7 copy.65
  (104 shorter events, 6.2 us)
Async XLA Ops:
  8.0 65.0 %copy-start = (bf16[256,1024]{1,0:T(8,128)(2,1)S(1)}, bf16[256,1024]{1,0:T(8,128)(2,1)}, u32[]{:S(2)}) copy-start(bf16[256,1024]{1,0:T(8,128)(2,1)} %param.13) | copy-start | bytes 1572868
  8.0 73.9 %copy-start.12 = (bf16[1,16,16,512]{3,2,1,0:T(8,128)(2,1)S(1)}, bf16[1,16,16,512]{3,2,1,0:T(8,128)(2,1)}, u32[]{:S(2)}) copy-start(bf16[1,16,16,512]{3,2,1,0:T(8,128)(2,1)} %param.10) | copy-start | bytes 786436
  8.0 65.6 %copy-start.21 = (f32[8,49]{1,0:T(8,128)S(1)}, f32[8,49]{1,0:T(8,128)}, u32[]{:S(2)}) copy-start(f32[8,49]{1,0:T(8,128)} %param.14) | copy-start | bytes 4708
  8.0 66.0 %copy-start.10 = (bf16[1,16,16,1024]{3,2,1,0:T(8,128)(2,1)S(1)}, bf16[1,16,16,1024]{3,2,1,0:T(8,128)(2,1)}, u32[]{:S(2)}) copy-start(bf16[1,16,16,1024]{3,2,1,0:T(8,128)(2,1)} %param.11) | copy-start | bytes 1572868
  8.0 136.3 %all-gather.2.cloned.1.call-start = ((), (), s32[]{:S(2)}) async-start(), calls=%async_computation.2 | async-start | bytes 1114112 | tf_op jit(solution)/shard_map/all_gather | solution.py:105
  9.0 90.8 %collective-permute-start.5 = (bf16[1,2,16,512]{3,2,1,0:T(8,128)(2,1)S(1)}, bf16[1,2,16,512]{3,2,1,0:T(8,128)(2,1)S(1)}, u32[]{:S(2)}, u32[]{:S(2)}) collective-permute-start(bf16[1,2,16,512]{3,2,1,0:T(8,128)(2,1)S(1)} %get-tuple-element.42), channel_id=1, source_target_pairs={{32,0},{64,32},{96,64},{128,96},{160,128},{192,160},{224,192},{256... | collective-permute-start | bytes 98312 | tf_op jit(solution)/shard_map/ppermute | solution.py:20
  20.8 76.9 %collective-permute-start.4 = (bf16[1,2,16,512]{3,2,1,0:T(8,128)(2,1)S(1)}, bf16[1,2,16,512]{3,2,1,0:T(8,128)(2,1)S(1)}, u32[]{:S(2)}, u32[]{:S(2)}) collective-permute-start(bf16[1,2,16,512]{3,2,1,0:T(8,128)(2,1)S(1)} %get-tuple-element.43), channel_id=1, source_target_pairs={{0,32},{32,64},{64,96},{96,128},{128,160},{160,192},{192,224},{224... | collective-permute-start | bytes 98312 | tf_op jit(solution)/shard_map/ppermute | solution.py:17
  23.5 67.0 %collective-permute-start.1 = (bf16[1,2,16,512]{3,2,1,0:T(8,128)(2,1)S(1)}, bf16[1,2,16,512]{3,2,1,0:T(8,128)(2,1)S(1)}, u32[]{:S(2)}, u32[]{:S(2)}) collective-permute-start(bf16[1,2,16,512]{3,2,1,0:T(8,128)(2,1)S(1)} %get-tuple-element.48), channel_id=1, source_target_pairs={{32,0},{64,32},{96,64},{128,96},{160,128},{192,160},{224,192},{256... | collective-permute-start | bytes 98312 | tf_op jit(solution)/shard_map/ppermute | solution.py:20
  29.6 57.2 %collective-permute-start = (bf16[1,2,16,512]{3,2,1,0:T(8,128)(2,1)S(1)}, bf16[1,2,16,512]{3,2,1,0:T(8,128)(2,1)S(1)}, u32[]{:S(2)}, u32[]{:S(2)}) collective-permute-start(bf16[1,2,16,512]{3,2,1,0:T(8,128)(2,1)S(1)} %get-tuple-element.49), channel_id=1, source_target_pairs={{0,32},{32,64},{64,96},{96,128},{128,160},{160,192},{192,224},{224... | collective-permute-start | bytes 98312 | tf_op jit(solution)/shard_map/ppermute | solution.py:17
  32.3 43.6 %collective-permute-start.12 = (bf16[1,2,16,512]{3,2,1,0:T(8,128)(2,1)S(1)}, bf16[1,2,16,512]{3,2,1,0:T(8,128)(2,1)S(1)}, u32[]{:S(2)}, u32[]{:S(2)}) collective-permute-start(bf16[1,2,16,512]{3,2,1,0:T(8,128)(2,1)S(1)} %get-tuple-element.45), channel_id=1, source_target_pairs={{0,32},{32,64},{64,96},{96,128},{128,160},{160,192},{192,224},{224... | collective-permute-start | bytes 98312 | tf_op jit(solution)/shard_map/ppermute | solution.py:17
  71.4 19.1 %copy-start.13 = (bf16[1,16,16,512]{3,2,1,0:T(8,128)(2,1)S(1)}, bf16[1,16,16,512]{3,2,1,0:T(8,128)(2,1)}, u32[]{:S(2)}) copy-start(bf16[1,16,16,512]{3,2,1,0:T(8,128)(2,1)} %param.9) | copy-start | bytes 786436
  72.2 207.7 %reduce-scatter.5.cloned.1.call-start = ((), (), s32[]{:S(2)}) async-start(), calls=%async_computation.3 | async-start | bytes 2162688 | tf_op jit(solution)/shard_map/reduce_scatter | solution.py:166
  73.3 26.4 %copy-start.14 = (bf16[1,16,16,512]{3,2,1,0:T(8,128)(2,1)S(1)}, bf16[1,16,16,512]{3,2,1,0:T(8,128)(2,1)}, u32[]{:S(2)}) copy-start(bf16[1,16,16,512]{3,2,1,0:T(8,128)(2,1)} %param.8) | copy-start | bytes 786436
  73.5 0.6 copy-start.18
  74.2 35.9 %copy-start.16 = (pred[5,4]{1,0:T(8,128)(4,1)}, pred[5,4]{1,0:T(8,128)(4,1)S(1)}, u32[]{:S(2)}) copy-start(pred[5,4]{1,0:T(8,128)(4,1)S(1)} %fusion.16) | copy-start | bytes 64
  75.9 7.6 %collective-permute-start.13 = (bf16[1,2,16,512]{3,2,1,0:T(8,128)(2,1)S(1)}, bf16[1,2,16,512]{3,2,1,0:T(8,128)(2,1)S(1)}, u32[]{:S(2)}, u32[]{:S(2)}) collective-permute-start(bf16[1,2,16,512]{3,2,1,0:T(8,128)(2,1)S(1)} %get-tuple-element.44), channel_id=1, source_target_pairs={{32,0},{64,32},{96,64},{128,96},{160,128},{192,160},{224,192},{256... | collective-permute-start | bytes 98312 | tf_op jit(solution)/shard_map/ppermute | solution.py:20
  83.5 0.7 copy-start.8
  84.9 33.4 %collective-permute-start.14 = (bf16[1,20,2,512]{3,2,1,0:T(2,128)(2,1)}, bf16[1,20,2,512]{3,2,1,0:T(2,128)(2,1)S(1)}, u32[]{:S(2)}, u32[]{:S(2)}) collective-permute-start(bf16[1,20,2,512]{3,2,1,0:T(2,128)(2,1)} %get-tuple-element.36), channel_id=1, source_target_pairs={{0,1},{1,2},{2,3},{3,4},{4,5},{5,6},{6,7},{7,8},{8,9},{9,10},{10,1... | collective-permute-start | bytes 122888 | tf_op jit(solution)/shard_map/ppermute | solution.py:17
  86.8 31.5 %collective-permute-start.15 = (bf16[1,20,2,512]{3,2,1,0:T(2,128)(2,1)}, bf16[1,20,2,512]{3,2,1,0:T(2,128)(2,1)}, u32[]{:S(2)}, u32[]{:S(2)}) collective-permute-start(bf16[1,20,2,512]{3,2,1,0:T(2,128)(2,1)} %get-tuple-element.37), channel_id=1, source_target_pairs={{1,0},{2,1},{3,2},{4,3},{5,4},{6,5},{7,6},{8,7},{9,8},{10,9},{11,1... | collective-permute-start | bytes 122888 | tf_op jit(solution)/shard_map/ppermute | solution.py:20
  90.6 16.5 %collective-permute-start.2 = (bf16[1,20,2,512]{3,2,1,0:T(2,128)(2,1)S(1)}, bf16[1,20,2,512]{3,2,1,0:T(2,128)(2,1)S(1)}, u32[]{:S(2)}, u32[]{:S(2)}) collective-permute-start(bf16[1,20,2,512]{3,2,1,0:T(2,128)(2,1)S(1)} %get-tuple-element.40), channel_id=1, source_target_pairs={{0,1},{1,2},{2,3},{3,4},{4,5},{5,6},{6,7},{7,8},{8,9},{9,10},{10,1... | collective-permute-start | bytes 122888 | tf_op jit(solution)/shard_map/ppermute | solution.py:17
  97.8 11.3 %collective-permute-start.3 = (bf16[1,20,2,512]{3,2,1,0:T(2,128)(2,1)S(1)}, bf16[1,20,2,512]{3,2,1,0:T(2,128)(2,1)S(1)}, u32[]{:S(2)}, u32[]{:S(2)}) collective-permute-start(bf16[1,20,2,512]{3,2,1,0:T(2,128)(2,1)S(1)} %get-tuple-element.41), channel_id=1, source_target_pairs={{1,0},{2,1},{3,2},{4,3},{5,4},{6,5},{7,6},{8,7},{9,8},{10,9},{11,1... | collective-permute-start | bytes 122888 | tf_op jit(solution)/shard_map/ppermute | solution.py:20
  99.9 10.3 %collective-permute-start.6 = (bf16[1,20,2,512]{3,2,1,0:T(2,128)(2,1)S(1)}, bf16[1,20,2,512]{3,2,1,0:T(2,128)(2,1)S(1)}, u32[]{:S(2)}, u32[]{:S(2)}) collective-permute-start(bf16[1,20,2,512]{3,2,1,0:T(2,128)(2,1)S(1)} %get-tuple-element.34), channel_id=1, source_target_pairs={{0,1},{1,2},{2,3},{3,4},{4,5},{5,6},{6,7},{7,8},{8,9},{9,10},{10,1... | collective-permute-start | bytes 122888 | tf_op jit(solution)/shard_map/ppermute | solution.py:17
  107.1 8.0 %collective-permute-start.7 = (bf16[1,20,2,512]{3,2,1,0:T(2,128)(2,1)S(1)}, bf16[1,20,2,512]{3,2,1,0:T(2,128)(2,1)S(1)}, u32[]{:S(2)}, u32[]{:S(2)}) collective-permute-start(bf16[1,20,2,512]{3,2,1,0:T(2,128)(2,1)S(1)} %get-tuple-element.35), channel_id=1, source_target_pairs={{1,0},{2,1},{3,2},{4,3},{5,4},{6,5},{7,6},{8,7},{9,8},{10,9},{11,1... | collective-permute-start | bytes 122888 | tf_op jit(solution)/shard_map/ppermute | solution.py:20
  117.8 1.0 copy-start.9
  123.6 3.7 %copy-start.6 = (bf16[5,4,5,4,8,64]{5,3,1,4,2,0:T(4,128)(2,1)S(1)}, bf16[5,4,5,4,8,64]{5,3,1,4,2,0:T(4,128)(2,1)}, u32[]{:S(2)}) copy-start(bf16[5,4,5,4,8,64]{5,3,1,4,2,0:T(4,128)(2,1)} %copy.57) | copy-start | bytes 1228804
  133.9 20.2 %copy-start.11 = (bf16[1,16,16,1024]{3,2,1,0:T(8,128)(2,1)S(1)}, bf16[1,16,16,1024]{3,2,1,0:T(8,128)(2,1)}, u32[]{:S(2)}) copy-start(bf16[1,16,16,1024]{3,2,1,0:T(8,128)(2,1)} %param.11) | copy-start | bytes 1572868
  133.9 215.9 %reduce-scatter.7.cloned.1.call-start = ((), (), s32[]{:S(2)}) async-start(), calls=%async_computation.4 | async-start | bytes 139264
  144.3 9.8 %copy-start.5 = (bf16[512,1024]{1,0:T(8,128)(2,1)S(1)}, bf16[512,1024]{1,0:T(8,128)(2,1)}, u32[]{:S(2)}) copy-start(bf16[512,1024]{1,0:T(8,128)(2,1)} %all-gather.2.cloned.1.call-done) | copy-start | bytes 3145732
  146.1 8.5 %collective-permute-start.8 = (bf16[1,2,16,512]{3,2,1,0:T(8,128)(2,1)S(1)}, bf16[1,2,16,512]{3,2,1,0:T(8,128)(2,1)S(1)}, u32[]{:S(2)}, u32[]{:S(2)}) collective-permute-start(bf16[1,2,16,512]{3,2,1,0:T(8,128)(2,1)S(1)} %get-tuple-element.46), channel_id=1, source_target_pairs={{0,32},{32,64},{64,96},{96,128},{128,160},{160,192},{192,224},{224... | collective-permute-start | bytes 98312 | tf_op jit(solution)/shard_map/ppermute | solution.py:17
  148.6 7.1 %collective-permute-start.9 = (bf16[1,2,16,512]{3,2,1,0:T(8,128)(2,1)S(1)}, bf16[1,2,16,512]{3,2,1,0:T(8,128)(2,1)S(1)}, u32[]{:S(2)}, u32[]{:S(2)}) collective-permute-start(bf16[1,2,16,512]{3,2,1,0:T(8,128)(2,1)S(1)} %get-tuple-element.47), channel_id=1, source_target_pairs={{32,0},{64,32},{96,64},{128,96},{160,128},{192,160},{224,192},{256... | collective-permute-start | bytes 98312 | tf_op jit(solution)/shard_map/ppermute | solution.py:20
  154.6 9.1 %copy-start.17 = (pred[5,4]{1,0:T(8,128)(4,1)S(1)}, pred[5,4]{1,0:T(8,128)(4,1)}, u32[]{:S(2)}) copy-start(pred[5,4]{1,0:T(8,128)(4,1)} %copy-done.16) | copy-start | bytes 64
  155.7 5.8 %collective-permute-start.10 = (bf16[1,20,2,512]{3,2,1,0:T(2,128)(2,1)S(1)}, bf16[1,20,2,512]{3,2,1,0:T(2,128)(2,1)S(1)}, u32[]{:S(2)}, u32[]{:S(2)}) collective-permute-start(bf16[1,20,2,512]{3,2,1,0:T(2,128)(2,1)S(1)} %get-tuple-element.38), channel_id=1, source_target_pairs={{0,1},{1,2},{2,3},{3,4},{4,5},{5,6},{6,7},{7,8},{8,9},{9,10},{10,1... | collective-permute-start | bytes 122888 | tf_op jit(solution)/shard_map/ppermute | solution.py:17
  157.7 5.3 %collective-permute-start.11 = (bf16[1,20,2,512]{3,2,1,0:T(2,128)(2,1)S(1)}, bf16[1,20,2,512]{3,2,1,0:T(2,128)(2,1)S(1)}, u32[]{:S(2)}, u32[]{:S(2)}) collective-permute-start(bf16[1,20,2,512]{3,2,1,0:T(2,128)(2,1)S(1)} %get-tuple-element.39), channel_id=1, source_target_pairs={{1,0},{2,1},{3,2},{4,3},{5,4},{6,5},{7,6},{8,7},{9,8},{10,9},{11,1... | collective-permute-start | bytes 122888 | tf_op jit(solution)/shard_map/ppermute | solution.py:20
  163.7 1.5 copy-start.1
  163.7 1.4 copy-start.15
  164.3 1.5 copy-start.7
  167.4 2.8 copy-start.2
  173.7 0.9 copy-start.19
  173.7 103.8 %copy-start.3 = (bf16[20,20,512]{2,1,0:T(8,128)(2,1)S(1)}, bf16[20,20,512]{2,1,0:T(8,128)(2,1)}, u32[]{:S(2)}) copy-start(bf16[20,20,512]{2,1,0:T(8,128)(2,1)} %reshape.326) | copy-start | bytes 1228804
  173.7 104.6 %copy-start.4 = (bf16[20,20,512]{2,1,0:T(8,128)(2,1)S(1)}, bf16[20,20,512]{2,1,0:T(8,128)(2,1)}, u32[]{:S(2)}) copy-start(bf16[20,20,512]{2,1,0:T(8,128)(2,1)} %reshape.322) | copy-start | bytes 1228804
  174.1 107.5 %copy-start.20 = (f32[16]{0:T(128)S(1)}, f32[16]{0:T(128)}, u32[]{:S(2)}) copy-start(f32[16]{0:T(128)} %dynamic-slice) | copy-start | bytes 196
Sparse Core Ops, SparseCore 0:
  72.3 71.9 all-gather.1
  281.7 68.0 reduce-scatter.6
Sparse Core Ops, SparseCore 1:
  134.0 127.9 reduce-scatter.4
where the time goes:
time: 360 us; the launch traced here: 359 us
  blocking collectives  139 us (39%)
  waiting for transfers between devices  87.1 us (24%)
  starting transfers between devices  67.3 us (19%)
  local copies, waits for them, and re-layouts  27.4 us (8%)
  between operations  16.9 us (5%)
  matrix products  14.9 us (4%)
  other arithmetic  6.12 us (2%)
    psum x1, blocking collectives, body(): lax.psum((gate_part, bias_terms * factor), ('lat', 'lon'))  103 us
    unnamed x4, waiting for transfers between devices  67.6 us
    ppermute x8, starting transfers between devices, extended(): lax.ppermute(lax.slice_in_dim(block, 0, width, axis=dim), axis, backward)  40.7 us
    all_gather x1, blocking collectives, body(): row_band = lax.all_gather(out_weight, 'lon', axis=1, tiled=True)  36.4 us
    ppermute x8, starting transfers between devices, extended(): lax.ppermute(lax.slice_in_dim(block, block.shape[dim] - width, None, axis...  26.4 us
    all_gather x1, waiting for transfers between devices, body(): full_weight = lax.all_gather(row_band, 'lat', axis=0, tiled=True)  10.4 us
    ppermute x8, waiting for transfers between devices, extended(): lax.ppermute(lax.slice_in_dim(block, 0, width, axis=dim), axis, backward)  9.04 us
  transfers between devices with their start and end apart: 19, of which 6 were waited for; matrix products, arithmetic and copies ran while one was open for 12% of the time, Pallas kernels for 0%

commit v1 on v0

v1 whole, which is shorter than its diff:
```python
import functools
import math

import jax
import jax.numpy as jnp
import numpy as np
from jax import lax
from jax.experimental import pallas as pl
from jax.experimental.pallas import tpu as pltpu
from jax.sharding import PartitionSpec as P

SHIFT = 2
XL = 2
XH = 2
NEG = -1e9
MESH = pl.DeviceIdType.MESH
BF = jnp.bfloat16
F32 = jnp.float32


def strip_tables():
    first = np.zeros((2, 7, 16, 256), np.float32)
    second = np.zeros((2, 7, 16, 256), np.float32)
    for way, col0 in ((0, 14), (1, 0)):
        for block in range(7):
            for r in range(4):
                if block < 5:
                    row = 4 * block + r - SHIFT
                elif block == 5:
                    row = 14 + r if r < 2 else -1
                else:
                    row = r - 2 if r >= 2 else -1
                if not 0 <= row < 16:
                    continue
                for c in range(2):
                    token = row * 16 + col0 + c
                    low = r * 2 + c
                    first[way, block, low if way == 0 else low + 8, token] = 1.0
                    second[way, block, low + 8 if way == 0 else low, token] = 1.0
    return first.reshape(224, 256), second.reshape(224, 256)


def slot_places(swap):
    places = [(i // 16, i % 16 + SHIFT) for i in range(64)]
    left = [(r, c) for r in range(4) for c in range(2)]
    right = [(r, 18 + c) for r in range(4) for c in range(2)]
    return places + (right + left if swap else left + right)


def place_tables():
    queries, keys = slot_places(False), slot_places(True)
    offsets = np.full((80, 80), 49, np.int32)
    for k, (kr, kc) in enumerate(keys):
        for q, (qr, qc) in enumerate(queries):
            if kc // 4 == qc // 4:
                offsets[k, q] = 7 * (qr - kr + 3) + (qc % 4 - kc % 4 + 3)
    fold_keys = np.zeros((32, 160), np.float32)
    for head in range(2):
        for k, (kr, kc) in enumerate(keys):
            fold_keys[head * 16 + kr * 4 + kc % 4, head * 80 + k] = 1.0
    fold_queries = np.zeros((80, 16), np.float32)
    for q, (qr, qc) in enumerate(queries):
        fold_queries[q, qr * 4 + qc % 4] = 1.0
    return offsets, fold_keys, fold_queries


def dot(a, b, ca, cb, precision=None):
    return lax.dot_general(
        a, b, (((ca,), (cb,)), ((), ())), precision=precision, preferred_element_type=F32
    )


def kernel(
    nz,
    ny,
    hd,
    model,
    factor,
    q_in,
    k_in,
    v_in,
    og_in,
    w_in,
    tw_in,
    rel_in,
    t_in,
    selq,
    selk,
    offs,
    foldk,
    foldq,
    dq_out,
    dk_out,
    dv_out,
    wg_out,
    tg_out,
    bg_out,
    xe,
    lrx,
    snd,
    rcv,
    slab,
    yb,
    wz,
    wf,
    ge,
    gate_ref,
    bias_ref,
    prob_ref,
    mb,
    rc,
    mc,
    rx,
    mz,
    rz,
    ry,
    rsum,
    dqs,
    dks,
    dvs,
    bterm,
    ay,
    az,
    ax,
    load_sem,
    out_sem,
    halo_s,
    halo_r,
    agy_s,
    agy_r,
    agz_s,
    agz_r,
    agx_s,
    agx_r,
    agc_s,
    agc_r,
    rsc_s,
    rsc_r,
    rsx_s,
    rsx_r,
    rsz_s,
    rsz_r,
    rsy_s,
    rsy_r,
    ary_s,
    ary_r,
    arz_s,
    arz_r,
    arx_s,
    arx_r,
):
    lat = lax.axis_index("lat")
    lon = lax.axis_index("lon")
    nlat, nlon = XL * nz, XH * ny * 2
    xl, z = lat // nz, lat % nz
    xh, y, core = lon // (2 * ny), (lon // 2) % ny, lon % 2
    half = model // XH
    slabs = hd // 128
    heads = hd // 64
    width = 3 * hd + model
    og0 = 3 * hd
    groups = ny // 2

    def at(xl_, z_, xh_, y_, core_):
        return (xl_ * nz + z_, xh_ * 2 * ny + y_ * 2 + core_)

    zs = [(d, lax.rem(z + d, nz), lax.rem(z - d + nz, nz)) for d in range(1, nz)]
    xs = [(a, b) for a in range(XL) for b in range(XH) if a + b]
    ys = [
        (dy, dc, lax.rem(y + dy, ny), lax.rem(y - dy + ny, ny), core ^ dc)
        for dy in range(ny)
        for dc in range(2)
        if dy + dc
    ]
    up, down = lax.rem(lat + nlat - 1, nlat), lax.rem(lat + 1, nlat)
    left, right = lax.rem(lon + nlon - 1, nlon), lax.rem(lon + 1, nlon)

    def remote(src, dst, send, recv, device):
        return pltpu.make_async_remote_copy(
            src_ref=src,
            dst_ref=dst,
            send_sem=send,
            recv_sem=recv,
            device_id=device,
            device_id_type=MESH,
        )

    loads = [
        pltpu.make_async_copy(q_in.at[0], xe.at[2:18, :, 0:hd], load_sem.at[0]),
        pltpu.make_async_copy(k_in.at[0], xe.at[2:18, :, hd : 2 * hd], load_sem.at[1]),
        pltpu.make_async_copy(v_in.at[0], xe.at[2:18, :, 2 * hd : og0], load_sem.at[2]),
        pltpu.make_async_copy(og_in.at[0], xe.at[2:18, :, og0:width], load_sem.at[3]),
    ]
    for load in loads:
        load.start()

    barrier = pltpu.get_barrier_semaphore()
    peers = [at(xl, z_, xh, y, core) for _, z_, _ in zs]
    peers += [at(xl ^ a, z, xh ^ b, y, core) for a, b in xs]
    peers += [at(xl, z, xh, y_, core_) for _, _, y_, _, core_ in ys]
    peers += [(up, lon), (down, lon)]
    peers += [(i, j) for j in (left, right) for i in (lat, up, down)]
    for peer in peers:
        pl.semaphore_signal(barrier, inc=1, device_id=peer, device_id_type=MESH)

    lane = lax.broadcasted_iota(jnp.int32, (32, 128), 1)
    row = lax.broadcasted_iota(jnp.int32, (32, 128), 0)
    lane0 = lax.rem(lon, 4) * 32
    spread = (lane == row + lane0).astype(F32).astype(BF)
    slab[...] = dot(w_in[...], spread, 1, 0).astype(BF).reshape(2, 16, 128)
    yb[y, core] = slab[core]

    for load in loads:
        load.wait()

    fields = [
        xe[2:18, :, 0:hd].reshape(256, hd),
        xe[2:18, :, hd : 2 * hd].reshape(256, hd),
        xe[2:18, :, og0 : og0 + half].reshape(256, hd),
        xe[2:18, :, 2 * hd : og0].reshape(256, hd),
        xe[2:18, :, og0 + half : width].reshape(256, hd),
    ]
    sq, sk = selq[...], selk[...]
    snd[:, :, 0] = (
        (dot(sq, fields[0], 1, 0) + dot(sk, fields[1], 1, 0)).astype(BF).reshape(2, 7, 16, hd)
    )
    snd[:, :, 1] = (
        (dot(sq, fields[2], 1, 0) + dot(sk, fields[3], 1, 0)).astype(BF).reshape(2, 7, 16, hd)
    )
    snd[:, :, 2] = dot(sq, fields[4], 1, 0).astype(BF).reshape(2, 7, 16, hd)

    pl.semaphore_wait(barrier, len(peers))

    def agy(dy, dc, y_, core_, yslot, cslot):
        return remote(
            slab.at[core_],
            yb.at[yslot, cslot],
            agy_s.at[dy, dc],
            agy_r.at[dy, dc],
            at(xl, z, xh, y_, core_),
        )

    agy_sent = [agy(dy, dc, y_, core_, y, core) for dy, dc, y_, _, core_ in ys]
    for copy in agy_sent:
        copy.start()

    halos = [
        remote(xe.at[16:18], xe.at[0:2], halo_s.at[0], halo_r.at[0], (down, lon)),
        remote(xe.at[2:4], xe.at[18:20], halo_s.at[1], halo_r.at[1], (up, lon)),
        remote(snd.at[0, 0:5], rcv.at[0, 0:5], halo_s.at[2], halo_r.at[2], (lat, right)),
        remote(snd.at[1, 0:5], rcv.at[1, 0:5], halo_s.at[3], halo_r.at[3], (lat, left)),
        remote(snd.at[0, 5], rcv.at[0, 5], halo_s.at[4], halo_r.at[4], (down, right)),
        remote(snd.at[0, 6], rcv.at[0, 6], halo_s.at[5], halo_r.at[5], (up, right)),
        remote(snd.at[1, 5], rcv.at[1, 5], halo_s.at[6], halo_r.at[6], (down, left)),
        remote(snd.at[1, 6], rcv.at[1, 6], halo_s.at[7], halo_r.at[7], (up, left)),
    ]
    for copy in halos:
        copy.start()

    tval = t_in[0].astype(F32)
    half_emb = tw_in.shape[0] // 2
    decay = -math.log(10000.0)
    freq = lax.broadcasted_iota(jnp.int32, (16, half_emb), 1).astype(F32)
    angle = tval * jnp.exp(decay * freq / half_emb)
    emb = jnp.concatenate([jnp.cos(angle), jnp.sin(angle)], axis=1)
    emb_hi = emb.astype(BF).astype(F32)
    emb_mid = (emb - emb_hi).astype(BF).astype(F32)
    emb_lo = emb - emb_hi - emb_mid
    emb_row = lax.broadcasted_iota(jnp.int32, (16, 2 * half_emb), 0)
    parts = jnp.where(
        emb_row == 0,
        emb_hi,
        jnp.where(emb_row == 1, emb_mid, jnp.where(emb_row == 2, emb_lo, 0.0)),
    ).astype(BF)
    gate = jnp.sum(dot(parts, tw_in[...], 1, 0), axis=0, keepdims=True)
    gate_ref[...] = jnp.broadcast_to(gate, (8, model))

    def bias_rows(i, carry):
        rows = pl.ds(pl.multiple_of(i * 16, 16), 16)
        code = offs[rows, :]
        acc = [jnp.full((16, 80), NEG, F32) for _ in range(heads)]
        for o in range(49):
            hit = code == o
            acc = [jnp.where(hit, rel_in[h, o], acc[h]) for h in range(heads)]
        for h in range(heads):
            bias_ref[h, rows, :] = acc[h]
        return carry

    lax.fori_loop(0, 5, bias_rows, 0)

    for dy, dc, _, ysrc, csrc in ys:
        agy(dy, dc, ysrc, csrc, ysrc, csrc).wait_recv()
    for g in range(groups):
        pair = yb[2 * g, 0] + yb[2 * g, 1] + (yb[2 * g + 1, 0] + yb[2 * g + 1, 1])
        wz[z, :, g * 128 : (g + 1) * 128] = pair

    def agz(d, z_, zslot):
        return remote(
            wz.at[zslot], wz.at[zslot], agz_s.at[d], agz_r.at[d], at(xl, z_, xh, y, core)
        )

    agz_sent = [agz(d, z_, z) for d, z_, _ in zs]
    for copy in agz_sent:
        copy.start()

    for copy in halos:
        copy.wait_recv()
    top = (lax.broadcasted_iota(jnp.int32, (16, hd), 0) < 8).astype(F32).astype(BF)
    bot = (lax.broadcasted_iota(jnp.int32, (16, hd), 0) >= 8).astype(F32).astype(BF)
    for wi in range(5):
        got = []
        for m in range(3):
            pair = [rcv[0, wi, m], rcv[1, wi, m]]
            if wi == 0:
                pair = [pair[0] + rcv[0, 5, m], pair[1] + rcv[1, 5, m]]
            if wi == 4:
                pair = [pair[0] + rcv[0, 6, m], pair[1] + rcv[1, 6, m]]
            got.append(pair)
        lrx[wi, :, 0:hd] = got[0][0] * top + got[0][1] * bot
        lrx[wi, :, hd : 2 * hd] = got[0][1] * top + got[0][0] * bot
        lrx[wi, :, 2 * hd : og0] = got[1][1] * top + got[1][0] * bot
        lrx[wi, :, og0 : og0 + half] = got[1][0] * top + got[1][1] * bot
        lrx[wi, :, og0 + half : width] = got[2][0] * top + got[2][1] * bot

    lanes = lax.broadcasted_iota(jnp.int32, (80, 128), 1)
    mask0 = (lanes < 64).astype(F32).astype(BF)
    mask1 = (lanes >= 64).astype(F32).astype(BF)
    low_lanes = lax.broadcasted_iota(jnp.int32, (64, 128), 1) < 64

    def slot_row(shape, dim):
        i = lax.broadcasted_iota(jnp.int32, shape, dim)
        return jnp.where(i < 64, i // 16, lax.rem(i, 8) // 2)

    key_row = slot_row((80, 80), 0)
    query_row = slot_row((1, 80), 1)
    query_lane = lax.broadcasted_iota(jnp.int32, (1, 80), 1)
    scale = 64 ** (-0.5)

    def group(wi, base, s):
        cols = pl.ds(pl.multiple_of(base + s * 128, 128), 128)
        own = xe[4 * wi : 4 * wi + 4, :, cols].reshape(64, 128)
        return jnp.concatenate([own, lrx[wi, :, cols]], axis=0)

    def both(x):
        return jnp.concatenate([x * mask0, x * mask1], axis=0)

    def global_row(wi, r):
        return lat * 16 - SHIFT + 4 * wi + r

    def forward(s, carry):
        attn = []
        bias = bias_ref[pl.ds(2 * s, 2)]
        for wi in range(5):
            q = group(wi, 0, s)
            kk = both(group(wi, hd, s))
            vv = both(group(wi, 2 * hd, s))
            score = (dot(kk, q, 1, 1) * scale).reshape(2, 80, 80) + bias
            if wi in (0, 4):
                rows = global_row(wi, key_row)
                score = jnp.where((rows >= 0) & (rows < nlat * 16), score, NEG)
            peak = jnp.max(score, axis=1, keepdims=True)
            expo = jnp.exp(score - peak)
            total = jnp.sum(expo, axis=1, keepdims=True)
            prob = expo / total
            if wi in (0, 4):
                rows = global_row(wi, query_row)
                keep = ((rows >= 0) & (rows < nlat * 16)).astype(F32)
                prob = prob * keep.reshape(1, 1, 80)
            prob = prob.reshape(160, 80)
            prob_ref[s, wi] = prob
            attn.append(dot(prob.astype(BF), vv, 0, 0)[0:64].astype(BF))
        attn = jnp.concatenate(attn, axis=0)[32:288]
        og = xe[2:18, :, og0:width].reshape(256, model)
        term = dot(attn, og, 0, 0).astype(BF).reshape(4, 2, 16, model)
        mb[pl.ds(4 * s, 4)] = term
        rsc(s).start()
        return carry

    def rsc(s):
        rows = pl.ds(4 * s, 4)
        return remote(
            mb.at[rows, 1 - core],
            rc.at[rows],
            rsc_s.at[s],
            rsc_r.at[s],
            at(xl, z, xh, y, 1 - core),
        )

    lax.fori_loop(0, slabs, forward, 0)

    for d, _, zsrc in zs:
        agz(d, zsrc, zsrc).wait_recv()

    def agx(a, b, xlslot, xhslot, xl_, xh_):
        return remote(
            wz,
            wf.at[pl.ds(xlslot * nz, nz), core, :, pl.ds(xhslot * half, half)],
            agx_s.at[a, b],
            agx_r.at[a, b],
            at(xl_, z, xh_, y, core),
        )

    agx_sent = [agx(a, b, xl, xh, xl ^ a, xh ^ b) for a, b in xs]
    for copy in agx_sent:
        copy.start()
    wf[pl.ds(xl * nz, nz), core, :, pl.ds(xh * half, half)] = wz[...]

    def agc(a, b):
        xl_, xh_ = xl ^ a, xh ^ b
        piece = wf.at[pl.ds(xl_ * nz, nz), core, :, pl.ds(xh_ * half, half)]
        return remote(piece, piece, agc_s.at[a, b], agc_r.at[a, b], at(xl, z, xh, y, 1 - core))

    def agc_got(a, b):
        piece = wf.at[pl.ds((xl ^ a) * nz, nz), 1 - core, :, pl.ds((xh ^ b) * half, half)]
        return remote(piece, piece, agc_s.at[a, b], agc_r.at[a, b], at(xl, z, xh, y, 1 - core))

    agc(0, 0).start()

    def core_sum(s, carry):
        rsc(s).wait_recv()
        rows = pl.ds(4 * s, 4)
        mc[rows] = (mb[rows, core].astype(F32) + rc[rows].astype(F32)).astype(BF)
        return carry

    lax.fori_loop(0, slabs, core_sum, 0)

    def rsx(a, b, slot_xl, slot_xh):
        xl_, xh_ = xl ^ a, xh ^ b
        return remote(
            mc.at[pl.ds(xl_ * nz, nz), :, pl.ds(xh_ * half, half)],
            rx.at[slot_xl * XH + slot_xh],
            rsx_s.at[a, b],
            rsx_r.at[a, b],
            at(xl_, z, xh_, y, core),
        )

    rsx_sent = [rsx(a, b, xl, xh) for a, b in xs]
    for copy in rsx_sent:
        copy.start()
    rx[xl * XH + xh] = mc[pl.ds(xl * nz, nz), :, pl.ds(xh * half, half)]

    gate_row = gate_ref[0:1, :]
    for wi in range(5):
        own = xe[4 * wi : 4 * wi + 4, :, og0:width].reshape(64, model)
        ge[wi, 0:64] = (own.astype(F32) * gate_row).astype(BF)
        ge[wi, 64:80] = (lrx[wi, :, og0:width].astype(F32) * gate_row).astype(BF)

    for a, b in xs:
        agx(a, b, xl ^ a, xh ^ b, xl ^ a, xh ^ b).wait_recv()
        agc(a, b).start()
    for a, b in [(0, 0)] + xs:
        agc_got(a, b).wait_recv()

    def backward(s, carry):
        weight = wf[pl.ds(4 * s, 4)].reshape(128, model)
        cot = dot(ge[...].reshape(400, model), weight, 1, 1).astype(BF)
        bias_sum = jnp.zeros((160, 80), F32)
        cols = pl.ds(pl.multiple_of(s * 128, 128), 128)
        for wi in range(5):
            q = group(wi, 0, s)
            kk = both(group(wi, hd, s))
            vv = both(group(wi, 2 * hd, s))
            c = cot[80 * wi : 80 * wi + 80]
            prob = prob_ref[s, wi].reshape(2, 80, 80)
            dprob = dot(vv, c, 1, 1).reshape(2, 80, 80)
            inner = jnp.sum(prob * dprob, axis=1, keepdims=True)
            dscore = (prob * (dprob - inner)).reshape(160, 80)
            if wi in (0, 4):
                first, last = (32, 64) if wi == 0 else (0, 32)
            else:
                first, last = 0, 64
            mine = (query_lane >= first) & (query_lane < last)
            bias_sum = bias_sum + jnp.where(mine, dscore, 0.0)
            ds = dscore.astype(BF)
            pb = prob.reshape(160, 80).astype(BF)
            dq = dot(ds, kk, 0, 0)[0:64] * scale
            own_ds = jnp.concatenate([ds[0:64], ds[80:144]], axis=0)
            own_pb = jnp.concatenate([pb[0:64], pb[80:144]], axis=0)
            dk = dot(own_ds, q, 1, 0) * scale
            dv = dot(own_pb, c, 1, 0)
            dk = jnp.where(low_lanes, dk[0:64], dk[64:128])
            dv = jnp.where(low_lanes, dv[0:64], dv[64:128])
            rows = slice(4 * wi, 4 * wi + 4)
            dqs[rows, :, cols] = dq.astype(BF).reshape(4, 16, 128)
            dks[rows, :, cols] = dk.astype(BF).reshape(4, 16, 128)
            dvs[rows, :, cols] = dv.astype(BF).reshape(4, 16, 128)
        high = lax.Precision.HIGHEST
        folded = dot(foldk[...], bias_sum, 1, 0, high)
        bterm[pl.ds(pl.multiple_of(32 * s, 32), 32), :] = dot(folded, foldq[...], 1, 0, high)
        return carry

    lax.fori_loop(0, slabs, backward, 0)

    outs = [
        pltpu.make_async_copy(dqs.at[2:18], dq_out.at[0], out_sem.at[0]),
        pltpu.make_async_copy(dks.at[2:18], dk_out.at[0], out_sem.at[1]),
        pltpu.make_async_copy(dvs.at[2:18], dv_out.at[0], out_sem.at[2]),
    ]
    for copy in outs:
        copy.start()

    for a, b in xs:
        rsx(a, b, xl ^ a, xh ^ b).wait_recv()
    for i in range(nz):
        total = rx[0, i].astype(F32)
        for j in range(1, XL * XH):
            total = total + rx[j, i].astype(F32)
        mz[i] = total.astype(BF)

    def rsz(d, z_, zslot):
        return remote(
            mz.at[z_], rz.at[zslot], rsz_s.at[d], rsz_r.at[d], at(xl, z_, xh, y, core)
        )

    rsz_sent = [rsz(d, z_, z) for d, z_, _ in zs]
    for copy in rsz_sent:
        copy.start()
    rz[z] = mz[z]

    term_row = lax.broadcasted_iota(jnp.int32, (16 * heads, 128), 0)
    key_place = lax.rem(term_row, 16)
    offset = lax.broadcasted_iota(jnp.int32, (16 * heads, 128), 1)
    by_offset = jnp.zeros((16 * heads, 128), F32)
    for p in range(16):
        goal = 7 * (p // 4 - key_place // 4 + 3) + (p % 4 - lax.rem(key_place, 4) + 3)
        by_offset = by_offset + jnp.where(offset == goal, bterm[:, p : p + 1], 0.0)
    by_offset = jnp.sum(by_offset.reshape(heads, 16, 128), axis=1)
    if heads < 8:
        by_offset = jnp.concatenate([by_offset, jnp.zeros((8 - heads, 128), F32)], axis=0)
    ay[y, core] = by_offset

    def ary(dy, dc, y_, core_, yslot, cslot):
        return remote(
            ay.at[yslot, cslot],
            ay.at[yslot, cslot],
            ary_s.at[dy, dc],
            ary_r.at[dy, dc],
            at(xl, z, xh, y_, core_),
        )

    ary_sent = [ary(dy, dc, y_, core_, y, core) for dy, dc, y_, _, core_ in ys]
    for copy in ary_sent:
        copy.start()

    for d, z_, zsrc in zs:
        rsz(d, zsrc, zsrc).wait_recv()
    total = rz[0].astype(F32)
    for j in range(1, nz):
        total = total + rz[j].astype(F32)
    rsum[...] = total.astype(BF)

    def rsy(dy, dc, y_, core_, yslot, cslot):
        cols = pl.ds(pl.multiple_of((y_ // 2) * 128, 128), 128)
        return remote(
            rsum.at[:, cols],
            ry.at[cslot, yslot],
            rsy_s.at[dy, dc],
            rsy_r.at[dy, dc],
            at(xl, z, xh, y_, core_),
        )

    rsy_sent = [rsy(dy, dc, y_, core_, y, core) for dy, dc, y_, _, core_ in ys]
    for copy in rsy_sent:
        copy.start()
    ry[core, y] = rsum[:, pl.ds(pl.multiple_of((y // 2) * 128, 128), 128)]

    for dy, dc, _, ysrc, csrc in ys:
        ary(dy, dc, ysrc, csrc, ysrc, csrc).wait_recv()
    bias_total = ay[0, 0] + ay[0, 1]
    for j in range(1, ny):
        bias_total = bias_total + ay[j, 0] + ay[j, 1]

    for dy, dc, _, ysrc, csrc in ys:
        rsy(dy, dc, ysrc, csrc, ysrc, csrc).wait_recv()
    block = []
    for c in range(2):
        total = ry[c, 0].astype(F32)
        for j in range(1, ny):
            total = total + ry[c, j].astype(F32)
        block.append(total)
    block = jnp.concatenate(block, axis=0)
    my_lanes = pl.ds(pl.multiple_of((lon // 4) * 128, 128), 128)
    gate_mine = gate_ref[0:1, my_lanes]
    back = lax.rem(128 - lane0, 128)
    weight_mine = wf[lat, :, :, my_lanes].reshape(32, 128).astype(F32)
    gate_term = jnp.sum(weight_mine * block, axis=0, keepdims=True)
    wg_out[...] = pltpu.roll(block * gate_mine * factor, back, 1)[:, 0:32]

    az[z, 0:8] = bias_total
    az[z, 8:16] = jnp.broadcast_to(gate_term, (8, 128))

    def arz(d, z_, zslot):
        return remote(
            az.at[zslot], az.at[zslot], arz_s.at[d], arz_r.at[d], at(xl, z_, xh, y, core)
        )

    arz_sent = [arz(d, z_, z) for d, z_, _ in zs]
    for copy in arz_sent:
        copy.start()

    emb_rows = 2 * half_emb // nlat
    index = lat * emb_rows + lax.broadcasted_iota(jnp.int32, (emb_rows, 128), 0)
    freq = lax.rem(index, half_emb).astype(F32)
    angle = tval * jnp.exp(decay * freq / half_emb)
    emb_mine = jnp.where(index < half_emb, jnp.cos(angle), jnp.sin(angle))

    for d, _, zsrc in zs:
        arz(d, zsrc, zsrc).wait_recv()
    total = az[0]
    for j in range(1, nz):
        total = total + az[j]
    ax[xl * XH + xh] = total

    def arx(a, b, slot):
        return remote(
            ax.at[slot], ax.at[slot], arx_s.at[a, b], arx_r.at[a, b], at(xl ^ a, z, xh ^ b, y, core)
        )

    arx_sent = [arx(a, b, xl * XH + xh) for a, b in xs]
    for copy in arx_sent:
        copy.start()
    for a, b in xs:
        arx(a, b, (xl ^ a) * XH + (xh ^ b)).wait_recv()
    bias_total = ax[0, 0:8] + ax[1, 0:8] + (ax[2, 0:8] + ax[3, 0:8])
    bg_out[...] = bias_total[0:heads, 0:49] * factor
    gate_sum = (ax[xh, 8:9] + ax[XH + xh, 8:9]) * factor
    gate_sum = pltpu.roll(jnp.broadcast_to(gate_sum, (8, 128)), back, 1)
    tg_out[...] = (emb_mine * gate_sum[0:1])[:, 0:32]

    for copy in outs:
        copy.wait()
    sent = agy_sent + halos + agz_sent + agx_sent + rsx_sent + rsz_sent
    sent += ary_sent + rsy_sent + arz_sent + arx_sent
    sent += [agc(a, b) for a, b in [(0, 0)] + xs]
    for copy in sent:
        copy.wait_send()
    lax.fori_loop(0, slabs, lambda s, c: (rsc(s).wait_send(), c)[1], 0)


def body(
    query_field, key_field, value_field, out_grad, out_weight, time_weight, rel_bias, timesteps
):
    frames, tile_rows, tile_cols, hd = query_field.shape
    model = out_grad.shape[3]
    heads = rel_bias.shape[0]
    nlat, nlon = lax.axis_size("lat"), lax.axis_size("lon")
    nz, ny = nlat // XL, nlon // (2 * XH)
    factor = 1.0 / math.sqrt(frames * tile_rows * nlat * tile_cols * nlon)
    half = model // XH
    slabs = hd // 128
    width = 3 * hd + model
    selq, selk = strip_tables()
    offs, foldk, foldq = place_tables()
    vmem = pl.BlockSpec(memory_space=pltpu.VMEM)
    smem = pl.BlockSpec(memory_space=pltpu.SMEM)
    hbm = pl.BlockSpec(memory_space=pl.ANY)
    dma = pltpu.SemaphoreType.DMA
    field = jax.ShapeDtypeStruct(query_field.shape, BF)
    sems = [dma((4,)), dma((3,))]
    for shape in (
        (8,),
        (ny, 2),
        (nz,),
        (XL, XH),
        (XL, XH),
        (slabs,),
        (XL, XH),
        (nz,),
        (ny, 2),
        (ny, 2),
        (nz,),
        (XL, XH),
    ):
        sems += [dma(shape), dma(shape)]
    return pl.pallas_call(
        functools.partial(kernel, nz, ny, hd, model, factor),
        out_shape=(
            field,
            field,
            field,
            jax.ShapeDtypeStruct(out_weight.shape, F32),
            jax.ShapeDtypeStruct((time_weight.shape[0] // nlat, model // nlon), F32),
            jax.ShapeDtypeStruct(rel_bias.shape, F32),
        ),
        in_specs=[hbm, hbm, hbm, hbm, vmem, vmem, smem, smem, vmem, vmem, vmem, vmem, vmem],
        out_specs=(hbm, hbm, hbm, vmem, vmem, vmem),
        scratch_shapes=[
            pltpu.VMEM((20, 16, width), BF),
            pltpu.VMEM((5, 16, width), BF),
            pltpu.VMEM((2, 7, 3, 16, hd), BF),
            pltpu.VMEM((2, 7, 3, 16, hd), BF),
            pltpu.VMEM((2, 16, 128), BF),
            pltpu.VMEM((ny, 2, 16, 128), BF),
            pltpu.VMEM((nz, 16, half), BF),
            pltpu.VMEM((nlat, 2, 16, model), BF),
            pltpu.VMEM((5, 80, model), BF),
            pltpu.VMEM((8, model), F32),
            pltpu.VMEM((heads, 80, 80), F32),
            pltpu.VMEM((slabs, 5, 160, 80), F32),
            pltpu.VMEM((nlat, 2, 16, model), BF),
            pltpu.VMEM((nlat, 16, model), BF),
            pltpu.VMEM((nlat, 16, model), BF),
            pltpu.VMEM((XL * XH, nz, 16, half), BF),
            pltpu.VMEM((nz, 16, half), BF),
            pltpu.VMEM((nz, 16, half), BF),
            pltpu.VMEM((2, ny, 16, 128), BF),
            pltpu.VMEM((16, half), BF),
            pltpu.VMEM((20, 16, hd), BF),
            pltpu.VMEM((20, 16, hd), BF),
            pltpu.VMEM((20, 16, hd), BF),
            pltpu.VMEM((16 * heads, 16), F32),
            pltpu.VMEM((ny, 2, 8, 128), F32),
            pltpu.VMEM((nz, 16, 128), F32),
            pltpu.VMEM((XL * XH, 16, 128), F32),
        ]
        + sems,
        compiler_params=pltpu.CompilerParams(
            collective_id=0, has_side_effects=True, vmem_limit_bytes=48 * 1024 * 1024
        ),
        cost_estimate=pl.CostEstimate(
            flops=2_000_000_000, bytes_accessed=4_000_000, transcendentals=1_000_000
        ),
    )(
        query_field,
        key_field,
        value_field,
        out_grad,
        out_weight,
        time_weight,
        rel_bias,
        timesteps,
        jnp.asarray(selq, BF),
        jnp.asarray(selk, BF),
        jnp.asarray(offs),
        jnp.asarray(foldk),
        jnp.asarray(foldq),
    )


def solution(mesh):
    tile = P(None, "lat", "lon", None)
    return jax.shard_map(
        body,
        mesh=mesh,
        in_specs=(tile, tile, tile, tile, P("lat", "lon"), P(), P(), P()),
        out_specs=(tile, tile, tile, P("lat", "lon"), P("lat", "lon"), P()),
        check_vma=False,
    )
```

time: 360 us -> 85.1 us (0.24)
  the two profiles are of different devices: /device:TPU:56 before, /device:TPU:1 now
where the time goes in v1:
time: 85.1 us; the launch traced here: 83.6 us
  Pallas kernels  68 us (80%)
  local copies, waits for them, and re-layouts  14.3 us (17%)
  between operations  1.31 us (2%)
    pallas_call x1, Pallas kernels, body(): pl.pallas_call(functools.partial(kernel, nz, ny, hd, model, factor), out_...  68 us
    unnamed x30, local copies, waits for them, and re-layouts  14.3 us

profile of v1, /device:TPU:1, one launch (start us, length us, event | category | flops | bytes accessed | tf_op | source)
XLA Modules:
  0.0 83.6 jit_solution(8317697465822529323)
XLA Ops:
  1.3 0.0 copy-start
  1.3 1.0 %copy-done = bf16[1,16,16,1024]{3,2,1,0:T(8,128)(2,1)S(1)} copy-done((bf16[1,16,16,1024]{3,2,1,0:T(8,128)(2,1)S(1)}, bf16[1,16,16,1024]{3,2,1,0:T(8,128)(2,1)}, u32[]{:S(2)}) %copy-start) | copy-done | bytes 524312
  2.3 0.0 copy-start.1
  2.3 1.0 %copy-done.1 = bf16[256,1024]{1,0:T(8,128)(2,1)S(1)} copy-done((bf16[256,1024]{1,0:T(8,128)(2,1)S(1)}, bf16[256,1024]{1,0:T(8,128)(2,1)}, u32[]{:S(2)}) %copy-start.1) | copy-done | bytes 524312
  3.4 0.0 copy-start.2
  3.4 0.9 %copy-done.2 = bf16[1,16,16,512]{3,2,1,0:T(8,128)(2,1)S(1)} copy-done((bf16[1,16,16,512]{3,2,1,0:T(8,128)(2,1)S(1)}, bf16[1,16,16,512]{3,2,1,0:T(8,128)(2,1)}, u32[]{:S(2)}) %copy-start.2) | copy-done | bytes 262168
  4.3 0.0 copy-start.3
  4.3 0.9 %copy-done.3 = bf16[1,16,16,512]{3,2,1,0:T(8,128)(2,1)S(1)} copy-done((bf16[1,16,16,512]{3,2,1,0:T(8,128)(2,1)S(1)}, bf16[1,16,16,512]{3,2,1,0:T(8,128)(2,1)}, u32[]{:S(2)}) %copy-start.3) | copy-done | bytes 262168
  5.3 0.0 copy-start.4
  5.3 0.9 %copy-done.4 = bf16[1,16,16,512]{3,2,1,0:T(8,128)(2,1)S(1)} copy-done((bf16[1,16,16,512]{3,2,1,0:T(8,128)(2,1)S(1)}, bf16[1,16,16,512]{3,2,1,0:T(8,128)(2,1)}, u32[]{:S(2)}) %copy-start.4) | copy-done | bytes 262168
  6.2 0.0 copy-start.5
  6.2 0.7 copy-done.5
  6.9 0.0 copy-start.6
  6.9 0.7 copy-done.6
  7.6 0.0 copy-start.7
  7.6 0.9 %copy-done.7 = bf16[224,256]{1,0:T(8,128)(2,1)S(1)} copy-done((bf16[224,256]{1,0:T(8,128)(2,1)S(1)}, bf16[224,256]{1,0:T(8,128)(2,1)}, u32[]{:S(2)}) %copy-start.7) | copy-done | bytes 114712
  8.5 0.0 copy-start.8
  8.5 0.9 %copy-done.8 = bf16[224,256]{1,0:T(8,128)(2,1)S(1)} copy-done((bf16[224,256]{1,0:T(8,128)(2,1)S(1)}, bf16[224,256]{1,0:T(8,128)(2,1)}, u32[]{:S(2)}) %copy-start.8) | copy-done | bytes 114712
  9.4 0.0 copy-start.9
  9.4 0.8 copy-done.9
  10.2 0.0 copy-start.10
  10.2 0.8 copy-done.10
  11.0 0.0 copy-start.11
  11.0 0.8 copy-done.11
  11.7 68.0 %shard_map.172 = (bf16[1,16,16,512]{3,2,1,0:T(8,128)(2,1)S(1)}, bf16[1,16,16,512]{3,2,1,0:T(8,128)(2,1)S(1)}, bf16[1,16,16,512]{3,2,1,0:T(8,128)(2,1)S(1)}, f32[...) custom-call(bf16[1,16,16,512]{3,2,1,0:T(8,128)(2,1)S(1)} %copy-done.2, ...), custom_call_target="tpu_custom_call" | custom-call | flops 2000000000 | bytes 4000000 | tf_op jit(solution)/shard_map/pallas_call | solution.py:675
  79.7 0.7 copy.26
  80.4 0.7 copy.27
  81.1 0.7 copy.28
  81.8 0.6 copy.29
  82.4 0.6 copy.30
  83.0 0.6 copy.31
Async XLA Ops:
  1.3 1.0 %copy-start = (bf16[1,16,16,1024]{3,2,1,0:T(8,128)(2,1)S(1)}, bf16[1,16,16,1024]{3,2,1,0:T(8,128)(2,1)}, u32[]{:S(2)}) copy-start(bf16[1,16,16,1024]{3,2,1,0:T(8,128)(2,1)} %og_in.1) | copy-start | bytes 1572868
  2.3 1.0 %copy-start.1 = (bf16[256,1024]{1,0:T(8,128)(2,1)S(1)}, bf16[256,1024]{1,0:T(8,128)(2,1)}, u32[]{:S(2)}) copy-start(bf16[256,1024]{1,0:T(8,128)(2,1)} %tw_in.1) | copy-start | bytes 1572868
  3.4 0.9 %copy-start.2 = (bf16[1,16,16,512]{3,2,1,0:T(8,128)(2,1)S(1)}, bf16[1,16,16,512]{3,2,1,0:T(8,128)(2,1)}, u32[]{:S(2)}) copy-start(bf16[1,16,16,512]{3,2,1,0:T(8,128)(2,1)} %q_in.1) | copy-start | bytes 786436
  4.3 0.9 %copy-start.3 = (bf16[1,16,16,512]{3,2,1,0:T(8,128)(2,1)S(1)}, bf16[1,16,16,512]{3,2,1,0:T(8,128)(2,1)}, u32[]{:S(2)}) copy-start(bf16[1,16,16,512]{3,2,1,0:T(8,128)(2,1)} %k_in.1) | copy-start | bytes 786436
  5.3 0.9 %copy-start.4 = (bf16[1,16,16,512]{3,2,1,0:T(8,128)(2,1)S(1)}, bf16[1,16,16,512]{3,2,1,0:T(8,128)(2,1)}, u32[]{:S(2)}) copy-start(bf16[1,16,16,512]{3,2,1,0:T(8,128)(2,1)} %v_in.1) | copy-start | bytes 786436
  6.2 0.7 copy-start.5
  6.9 0.7 copy-start.6
  7.6 0.9 %copy-start.7 = (bf16[224,256]{1,0:T(8,128)(2,1)S(1)}, bf16[224,256]{1,0:T(8,128)(2,1)}, u32[]{:S(2)}) copy-start(bf16[224,256]{1,0:T(8,128)(2,1)} %constant.11.clone.selk) | copy-start | bytes 344068
  8.5 0.9 %copy-start.8 = (bf16[224,256]{1,0:T(8,128)(2,1)S(1)}, bf16[224,256]{1,0:T(8,128)(2,1)}, u32[]{:S(2)}) copy-start(bf16[224,256]{1,0:T(8,128)(2,1)} %constant.10.clone.selq) | copy-start | bytes 344068
  9.4 0.8 copy-start.9
  10.2 0.8 copy-start.10
  11.0 0.8 copy-start.11

commit v2 on v1

v2 whole, which is shorter than its diff:
```python
import functools
import math

import jax
import jax.numpy as jnp
import numpy as np
from jax import lax
from jax.experimental import pallas as pl
from jax.experimental.pallas import tpu as pltpu
from jax.sharding import PartitionSpec as P

SHIFT = 2
XL = 2
XH = 2
NEG = -1e9
VMEM_LIMIT = 60 * 1024 * 1024
MESH = pl.DeviceIdType.MESH
BF = jnp.bfloat16
F32 = jnp.float32


def strip_tables():
    first = np.zeros((2, 7, 16, 256), np.float32)
    second = np.zeros((2, 7, 16, 256), np.float32)
    for way, col0 in ((0, 14), (1, 0)):
        for block in range(7):
            for r in range(4):
                if block < 5:
                    row = 4 * block + r - SHIFT
                elif block == 5:
                    row = 14 + r if r < 2 else -1
                else:
                    row = r - 2 if r >= 2 else -1
                if not 0 <= row < 16:
                    continue
                for c in range(2):
                    token = row * 16 + col0 + c
                    low = r * 2 + c
                    first[way, block, low if way == 0 else low + 8, token] = 1.0
                    second[way, block, low + 8 if way == 0 else low, token] = 1.0
    return first.reshape(224, 256), second.reshape(224, 256)


def slot_places(swap):
    places = [(i // 16, i % 16 + SHIFT) for i in range(64)]
    left = [(r, c) for r in range(4) for c in range(2)]
    right = [(r, 18 + c) for r in range(4) for c in range(2)]
    return places + (right + left if swap else left + right)


def place_tables():
    queries, keys = slot_places(False), slot_places(True)
    offsets = np.full((80, 80), 49, np.int32)
    for k, (kr, kc) in enumerate(keys):
        for q, (qr, qc) in enumerate(queries):
            if kc // 4 == qc // 4:
                offsets[k, q] = 7 * (qr - kr + 3) + (qc % 4 - kc % 4 + 3)
    fold_keys = np.zeros((32, 160), np.float32)
    for head in range(2):
        for k, (kr, kc) in enumerate(keys):
            fold_keys[head * 16 + kr * 4 + kc % 4, head * 80 + k] = 1.0
    fold_queries = np.zeros((80, 16), np.float32)
    for q, (qr, qc) in enumerate(queries):
        fold_queries[q, qr * 4 + qc % 4] = 1.0
    return offsets, fold_keys, fold_queries


def dot(a, b, ca, cb, precision=None):
    return lax.dot_general(
        a, b, (((ca,), (cb,)), ((), ())), precision=precision, preferred_element_type=F32
    )


def kernel(
    nz,
    ny,
    hd,
    model,
    factor,
    q_in,
    k_in,
    v_in,
    og_in,
    w_hbm,
    tw_hbm,
    rel_hbm,
    t_hbm,
    sel_hbm,
    offs_hbm,
    foldk_hbm,
    foldq_hbm,
    dq_out,
    dk_out,
    dv_out,
    wg_hbm,
    tg_hbm,
    bg_hbm,
    w_in,
    tw_in,
    rel_in,
    t_in,
    sel,
    offs,
    foldk,
    foldq,
    xe,
    lrx,
    snd,
    rcv,
    snd2,
    rcv2,
    slab,
    slab_got,
    yb,
    wz,
    wf,
    ge,
    gate_ref,
    emb_mine,
    bias_ref,
    prob_ref,
    probb_ref,
    dscore_ref,
    cot_ref,
    mb,
    rc,
    mc,
    rx,
    mz,
    rz,
    rsum,
    ry,
    fin,
    dqs,
    dks,
    dvs,
    bterm,
    pay,
    ax,
    az,
    ay,
    wg_out,
    tg_out,
    bg_out,
    load_sem,
    out_sem,
    halo_s,
    halo_r,
    ag0_s,
    ag0_r,
    agy_s,
    agy_r,
    agz_s,
    agz_r,
    agx_s,
    agx_r,
    agc_s,
    agc_r,
    rsc_s,
    rsc_r,
    rsx_s,
    rsx_r,
    rsz_s,
    rsz_r,
    rsy_s,
    rsy_r,
    ary_s,
    ary_r,
    arz_s,
    arz_r,
    arx_s,
    arx_r,
):
    lat = lax.axis_index("lat")
    lon = lax.axis_index("lon")
    nlat, nlon = XL * nz, XH * ny * 2
    xl, z = lat // nz, lat % nz
    xh, y, core = lon // (2 * ny), (lon // 2) % ny, lon % 2
    half = model // XH
    slabs = hd // 128
    heads = hd // 64
    width = 3 * hd + model
    og0 = 3 * hd
    groups = ny // 2

    def at(xl_, z_, xh_, y_, core_):
        return (xl_ * nz + z_, xh_ * 2 * ny + y_ * 2 + core_)

    zs = [(d, lax.rem(z + d, nz), lax.rem(z - d + nz, nz)) for d in range(1, nz)]
    xs = [(a, b) for a in range(XL) for b in range(XH) if a + b]
    xcs = [(a, b, c) for a in range(XL) for b in range(XH) for c in range(2) if a + b + c]
    ys = [(d, lax.rem(y + d, ny), lax.rem(y - d + ny, ny)) for d in range(1, ny)]
    up, down = lax.rem(lat + nlat - 1, nlat), lax.rem(lat + 1, nlat)
    left, right = lax.rem(lon + nlon - 1, nlon), lax.rem(lon + 1, nlon)

    def remote(src, dst, send, recv, device):
        return pltpu.make_async_remote_copy(
            src_ref=src,
            dst_ref=dst,
            send_sem=send,
            recv_sem=recv,
            device_id=device,
            device_id_type=MESH,
        )

    barrier = pltpu.get_barrier_semaphore()
    sibling = at(xl, z, xh, y, 1 - core)
    peers = [sibling]
    peers += [at(xl, z, xh, y_, core) for _, y_, _ in ys]
    peers += [at(xl, z_, xh, y, core) for _, z_, _ in zs]
    peers += [at(xl ^ a, z, xh ^ b, y, core ^ c) for a, b, c in xcs]
    peers += [(up, lon), (down, lon)]
    peers += [(i, j) for j in (left, right) for i in (lat, up, down)]
    for peer in peers:
        pl.semaphore_signal(barrier, inc=1, device_id=peer, device_id_type=MESH)

    loads = [
        (w_hbm, w_in),
        (q_in.at[0], xe.at[2:18, :, 0:hd]),
        (k_in.at[0], xe.at[2:18, :, hd : 2 * hd]),
        (v_in.at[0], xe.at[2:18, :, 2 * hd : og0]),
        (og_in.at[0], xe.at[2:18, :, og0:width]),
        (sel_hbm, sel),
        (t_hbm, t_in),
        (tw_hbm, tw_in),
        (rel_hbm, rel_in),
        (offs_hbm, offs),
        (foldk_hbm, foldk),
        (foldq_hbm, foldq),
    ]
    loads = [pltpu.make_async_copy(a, b, load_sem.at[i]) for i, (a, b) in enumerate(loads)]
    for load in loads:
        load.start()

    lane = lax.broadcasted_iota(jnp.int32, (32, 128), 1)
    row = lax.broadcasted_iota(jnp.int32, (32, 128), 0)
    lane0 = lax.rem(lon, 4) * 32
    spread = (lane == row + lane0).astype(F32).astype(BF)
    loads[0].wait()
    slab[...] = dot(w_in[...], spread, 1, 0).astype(BF).reshape(2, 16, 128)
    pl.semaphore_wait(barrier, len(peers))
    ag0 = remote(slab.at[1 - core], slab_got, ag0_s.at[0], ag0_r.at[0], sibling)
    ag0.start()

    for load in loads[1:5]:
        load.wait()
    lat_qkv = [
        remote(
            xe.at[16:18, :, 0:og0], xe.at[0:2, :, 0:og0], halo_s.at[0], halo_r.at[0], (down, lon)
        ),
        remote(
            xe.at[2:4, :, 0:og0], xe.at[18:20, :, 0:og0], halo_s.at[1], halo_r.at[1], (up, lon)
        ),
    ]
    for copy in lat_qkv:
        copy.start()

    ag0.wait_recv()
    yb[y] = slab[core] + slab_got[...]

    def agy(d, y_, slot):
        return remote(yb.at[slot], yb.at[slot], agy_s.at[d], agy_r.at[d], at(xl, z, xh, y_, core))

    agy_sent = [agy(d, y_, y) for d, y_, _ in ys]
    for copy in agy_sent:
        copy.start()

    loads[5].wait()
    fields = [
        xe[2:18, :, 0:hd].reshape(256, hd),
        xe[2:18, :, hd : 2 * hd].reshape(256, hd),
        xe[2:18, :, og0 : og0 + half].reshape(256, hd),
        xe[2:18, :, 2 * hd : og0].reshape(256, hd),
        xe[2:18, :, og0 + half : width].reshape(256, hd),
    ]
    sq, sk = sel[0:224].astype(BF), sel[224:448].astype(BF)
    snd[:, :, 0] = (
        (dot(sq, fields[0], 1, 0) + dot(sk, fields[1], 1, 0)).astype(BF).reshape(2, 7, 16, hd)
    )
    snd[:, :, 1] = (
        (dot(sq, fields[2], 1, 0) + dot(sk, fields[3], 1, 0)).astype(BF).reshape(2, 7, 16, hd)
    )

    def strips(src, dst, base):
        devices = [
            (0, slice(0, 5), (lat, right)),
            (1, slice(0, 5), (lat, left)),
            (0, 5, (down, right)),
            (0, 6, (up, right)),
            (1, 5, (down, left)),
            (1, 6, (up, left)),
        ]
        return [
            remote(
                src.at[way, part],
                dst.at[way, part],
                halo_s.at[base + i],
                halo_r.at[base + i],
                device,
            )
            for i, (way, part, device) in enumerate(devices)
        ]

    lon_qkv = strips(snd, rcv, 2)
    for copy in lon_qkv:
        copy.start()
    snd2[...] = dot(sq, fields[4], 1, 0).astype(BF).reshape(2, 7, 16, hd)
    late = [
        remote(
            xe.at[16:18, :, og0:width],
            xe.at[0:2, :, og0:width],
            halo_s.at[8],
            halo_r.at[8],
            (down, lon),
        ),
        remote(
            xe.at[2:4, :, og0:width],
            xe.at[18:20, :, og0:width],
            halo_s.at[9],
            halo_r.at[9],
            (up, lon),
        ),
    ]
    late += strips(snd2, rcv2, 10)
    for copy in late:
        copy.start()

    for load in loads[6:]:
        load.wait()
    tval = t_in[0, 0].astype(F32)
    half_emb = tw_in.shape[0] // 2
    decay = -math.log(10000.0)
    freq = lax.broadcasted_iota(jnp.int32, (16, half_emb), 1).astype(F32)
    angle = tval * jnp.exp(decay * freq / half_emb)
    emb = jnp.concatenate([jnp.cos(angle), jnp.sin(angle)], axis=1)
    emb_hi = emb.astype(BF).astype(F32)
    emb_mid = (emb - emb_hi).astype(BF).astype(F32)
    emb_lo = emb - emb_hi - emb_mid
    emb_row = lax.broadcasted_iota(jnp.int32, (16, 2 * half_emb), 0)
    parts = jnp.where(
        emb_row == 0,
        emb_hi,
        jnp.where(emb_row == 1, emb_mid, jnp.where(emb_row == 2, emb_lo, 0.0)),
    ).astype(BF)
    gate = jnp.sum(dot(parts, tw_in[...], 1, 0), axis=0, keepdims=True)
    gate_ref[...] = jnp.broadcast_to(gate, (8, model))
    emb_rows = 2 * half_emb // nlat
    index = lat * emb_rows + lax.broadcasted_iota(jnp.int32, (emb_rows, 128), 0)
    freq = lax.rem(index, half_emb).astype(F32)
    angle = tval * jnp.exp(decay * freq / half_emb)
    emb_mine[...] = jnp.where(index < half_emb, jnp.cos(angle), jnp.sin(angle))

    def bias_rows(i, carry):
        rows = pl.ds(pl.multiple_of(i * 16, 16), 16)
        code = offs[rows, :]
        acc = [jnp.full((16, 80), NEG, F32) for _ in range(heads)]
        for o in range(49):
            hit = code == o
            acc = [jnp.where(hit, rel_in[h, o], acc[h]) for h in range(heads)]
        for h in range(heads):
            bias_ref[h, rows, :] = acc[h]
        return carry

    lax.fori_loop(0, 5, bias_rows, 0)

    for d, _, ysrc in ys:
        agy(d, ysrc, ysrc).wait_recv()
    for g in range(groups):
        wz[z, :, g * 128 : (g + 1) * 128] = yb[2 * g] + yb[2 * g + 1]

    def agz(d, z_, zslot):
        return remote(
            wz.at[zslot], wz.at[zslot], agz_s.at[d], agz_r.at[d], at(xl, z_, xh, y, core)
        )

    agz_sent = [agz(d, z_, z) for d, z_, _ in zs]
    for copy in agz_sent:
        copy.start()

    for copy in lat_qkv + lon_qkv:
        copy.wait_recv()
    top = (lax.broadcasted_iota(jnp.int32, (16, hd), 0) < 8).astype(F32).astype(BF)
    bot = (lax.broadcasted_iota(jnp.int32, (16, hd), 0) >= 8).astype(F32).astype(BF)
    for wi in range(5):
        got = []
        for m in range(2):
            pair = [rcv[0, wi, m], rcv[1, wi, m]]
            if wi == 0:
                pair = [pair[0] + rcv[0, 5, m], pair[1] + rcv[1, 5, m]]
            if wi == 4:
                pair = [pair[0] + rcv[0, 6, m], pair[1] + rcv[1, 6, m]]
            got.append(pair)
        lrx[wi, :, 0:hd] = got[0][0] * top + got[0][1] * bot
        lrx[wi, :, hd : 2 * hd] = got[0][1] * top + got[0][0] * bot
        lrx[wi, :, 2 * hd : og0] = got[1][1] * top + got[1][0] * bot
        lrx[wi, :, og0 : og0 + half] = got[1][0] * top + got[1][1] * bot

    lanes = lax.broadcasted_iota(jnp.int32, (80, 128), 1)
    mask0 = (lanes < 64).astype(F32).astype(BF)
    mask1 = (lanes >= 64).astype(F32).astype(BF)
    low_lanes = lax.broadcasted_iota(jnp.int32, (64, 128), 1) < 64

    def slot_row(shape, dim):
        i = lax.broadcasted_iota(jnp.int32, shape, dim)
        return jnp.where(i < 64, i // 16, lax.rem(i, 8) // 2)

    key_row = slot_row((80, 80), 0)
    query_row = slot_row((1, 80), 1)
    query_lane = lax.broadcasted_iota(jnp.int32, (1, 80), 1)
    scale = 64 ** (-0.5)

    def group(wi, base, s):
        cols = pl.ds(pl.multiple_of(base + s * 128, 128), 128)
        own = xe[4 * wi : 4 * wi + 4, :, cols].reshape(64, 128)
        return jnp.concatenate([own, lrx[wi, :, cols]], axis=0)

    def both(x):
        return jnp.concatenate([x * mask0, x * mask1], axis=0)

    def global_row(wi, r):
        return lat * 16 - SHIFT + 4 * wi + r

    def forward(s, carry):
        attn = []
        bias = bias_ref[pl.ds(2 * s, 2)]
        for wi in range(5):
            q = group(wi, 0, s)
            kk = both(group(wi, hd, s))
            vv = both(group(wi, 2 * hd, s))
            score = (dot(kk, q, 1, 1) * scale).reshape(2, 80, 80) + bias
            if wi in (0, 4):
                rows = global_row(wi, key_row)
                score = jnp.where((rows >= 0) & (rows < nlat * 16), score, NEG)
            peak = jnp.max(score, axis=1, keepdims=True)
            expo = jnp.exp(score - peak)
            inverse = 1.0 / jnp.sum(expo, axis=1, keepdims=True)
            if wi in (0, 4):
                rows = global_row(wi, query_row)
                keep = ((rows >= 0) & (rows < nlat * 16)).astype(F32)
                inverse = inverse * keep.reshape(1, 1, 80)
            prob = (expo * inverse).reshape(160, 80)
            prob_ref[s, wi] = prob
            prob_b = prob.astype(BF)
            probb_ref[s, wi] = prob_b
            attn.append(dot(prob_b, vv, 0, 0)[0:64].astype(BF))
        attn = jnp.concatenate(attn, axis=0)[32:288]
        og = xe[2:18, :, og0:width].reshape(256, model)
        term = dot(attn, og, 0, 0).astype(BF).reshape(4, 2, 16, model)
        mb[pl.ds(4 * s, 4)] = term
        rsc(s).start()
        return carry

    def rsc(s):
        rows = pl.ds(4 * s, 4)
        return remote(mb.at[rows, 1 - core], rc.at[rows], rsc_s.at[s], rsc_r.at[s], sibling)

    lax.fori_loop(0, slabs // 2, forward, 0)

    for d, _, zsrc in zs:
        agz(d, zsrc, zsrc).wait_recv()

    def agx(a, b, xlslot, xhslot, xl_, xh_):
        return remote(
            wz,
            wf.at[pl.ds(xlslot * nz, nz), core, :, pl.ds(xhslot * half, half)],
            agx_s.at[a, b],
            agx_r.at[a, b],
            at(xl_, z, xh_, y, core),
        )

    agx_sent = [agx(a, b, xl, xh, xl ^ a, xh ^ b) for a, b in xs]
    for copy in agx_sent:
        copy.start()
    wf[pl.ds(xl * nz, nz), core, :, pl.ds(xh * half, half)] = wz[...]

    def agc(a, b):
        xl_, xh_ = xl ^ a, xh ^ b
        piece = wf.at[pl.ds(xl_ * nz, nz), core, :, pl.ds(xh_ * half, half)]
        return remote(piece, piece, agc_s.at[a, b], agc_r.at[a, b], sibling)

    def agc_got(a, b):
        piece = wf.at[pl.ds((xl ^ a) * nz, nz), 1 - core, :, pl.ds((xh ^ b) * half, half)]
        return remote(piece, piece, agc_s.at[a, b], agc_r.at[a, b], sibling)

    agc(0, 0).start()
    lax.fori_loop(slabs // 2, slabs, forward, 0)

    def core_sum(s, carry):
        rsc(s).wait_recv()
        rows = pl.ds(4 * s, 4)
        mc[rows] = (mb[rows, core].astype(F32) + rc[rows].astype(F32)).astype(BF)
        return carry

    lax.fori_loop(0, slabs, core_sum, 0)

    def rsx(a, b, slot_xl, slot_xh):
        xl_, xh_ = xl ^ a, xh ^ b
        return remote(
            mc.at[pl.ds(xl_ * nz, nz), :, pl.ds(xh_ * half, half)],
            rx.at[slot_xl * XH + slot_xh],
            rsx_s.at[a, b],
            rsx_r.at[a, b],
            at(xl_, z, xh_, y, core),
        )

    rsx_sent = [rsx(a, b, xl, xh) for a, b in xs]
    for copy in rsx_sent:
        copy.start()
    rx[xl * XH + xh] = mc[pl.ds(xl * nz, nz), :, pl.ds(xh * half, half)]

    for copy in late:
        copy.wait_recv()
    gate_row = gate_ref[0:1, :]
    for wi in range(5):
        pair = [rcv2[0, wi], rcv2[1, wi]]
        if wi == 0:
            pair = [pair[0] + rcv2[0, 5], pair[1] + rcv2[1, 5]]
        if wi == 4:
            pair = [pair[0] + rcv2[0, 6], pair[1] + rcv2[1, 6]]
        lrx[wi, :, og0 + half : width] = pair[0] * top + pair[1] * bot
        own = xe[4 * wi : 4 * wi + 4, :, og0:width].reshape(64, model)
        ge[wi, 0:64] = (own.astype(F32) * gate_row).astype(BF)
        ge[wi, 64:80] = (lrx[wi, :, og0:width].astype(F32) * gate_row).astype(BF)

    for a, b in xs:
        agx(a, b, xl ^ a, xh ^ b, xl ^ a, xh ^ b).wait_recv()
        agc(a, b).start()
    for a, b in [(0, 0)] + xs:
        agc_got(a, b).wait_recv()

    def backward(s, gate_terms):
        weight = wf[pl.ds(4 * s, 4)].reshape(128, model)
        cot = dot(ge[...].reshape(400, model), weight, 1, 1).astype(BF)
        cot_ref[s] = cot
        bias_sum = jnp.zeros((160, 80), F32)
        for wi in range(5):
            vv = both(group(wi, 2 * hd, s))
            prob = prob_ref[s, wi].reshape(2, 80, 80)
            dprob = dot(vv, cot[80 * wi : 80 * wi + 80], 1, 1).reshape(2, 80, 80)
            inner = jnp.sum(prob * dprob, axis=1, keepdims=True)
            dscore = (prob * (dprob - inner)).reshape(160, 80)
            if wi in (0, 4):
                first, last = (32, 64) if wi == 0 else (0, 32)
            else:
                first, last = 0, 64
            mine = (query_lane >= first) & (query_lane < last)
            bias_sum = bias_sum + jnp.where(mine, dscore, 0.0)
            dscore_ref[s, wi] = dscore.astype(BF)
        folded = split_dot(foldk[...].astype(BF), bias_sum)
        bterm[pl.ds(pl.multiple_of(32 * s, 32), 32), :] = dot(
            folded, foldq[...], 1, 0, lax.Precision.HIGHEST
        )
        term = mb[pl.ds(4 * s, 4)].reshape(128, model)
        product = weight.astype(F32) * term.astype(F32)
        return gate_terms + jnp.sum(product.reshape(16, 8, model), axis=0)

    def split_dot(a, b):
        high = b.astype(BF)
        return dot(a, high, 1, 0) + dot(a, (b - high.astype(F32)).astype(BF), 1, 0)

    gate_terms = lax.fori_loop(0, slabs, backward, jnp.zeros((8, model), F32))
    gate_terms = jnp.sum(gate_terms, axis=0, keepdims=True)

    term_row = lax.broadcasted_iota(jnp.int32, (16 * heads, 128), 0)
    key_place = lax.rem(term_row, 16)
    offset = lax.broadcasted_iota(jnp.int32, (16 * heads, 128), 1)
    by_offset = jnp.zeros((16 * heads, 128), F32)
    for p in range(16):
        goal = 7 * (p // 4 - key_place // 4 + 3) + (p % 4 - lax.rem(key_place, 4) + 3)
        by_offset = by_offset + jnp.where(offset == goal, bterm[:, p : p + 1], 0.0)
    by_offset = jnp.sum(by_offset.reshape(heads, 16, 128), axis=1)
    if heads < 8:
        by_offset = jnp.concatenate([by_offset, jnp.zeros((8 - heads, 128), F32)], axis=0)
    for h in range(XH):
        pay[h, 0:8] = by_offset
        for g in range(8):
            first = h * half + min(g, groups - 1) * 128
            pay[h, 8 + g : 9 + g] = gate_terms[:, first : first + 128]

    def arx(a, b, c, slot_xl, slot_xh, slot_core, xl_, xh_, core_):
        return remote(
            pay.at[xh_],
            ax.at[slot_xl * XH + slot_xh, slot_core],
            arx_s.at[a, b, c],
            arx_r.at[a, b, c],
            at(xl_, z, xh_, y, core_),
        )

    arx_sent = [arx(a, b, c, xl, xh, core, xl ^ a, xh ^ b, core ^ c) for a, b, c in xcs]
    for copy in arx_sent:
        copy.start()
    ax[xl * XH + xh, core] = pay[xh]

    for a, b in xs:
        rsx(a, b, xl ^ a, xh ^ b).wait_recv()
    for i in range(nz):
        total = rx[0, i].astype(F32)
        for j in range(1, XL * XH):
            total = total + rx[j, i].astype(F32)
        mz[i] = total.astype(BF)

    def rsz(d, z_, zslot):
        return remote(mz.at[z_], rz.at[zslot], rsz_s.at[d], rsz_r.at[d], at(xl, z_, xh, y, core))

    rsz_sent = [rsz(d, z_, z) for d, z_, _ in zs]
    for copy in rsz_sent:
        copy.start()
    rz[z] = mz[z]

    def gradients(s, carry):
        cols = pl.ds(pl.multiple_of(s * 128, 128), 128)
        for wi in range(5):
            q = group(wi, 0, s)
            kk = both(group(wi, hd, s))
            c = cot_ref[s, 80 * wi : 80 * wi + 80]
            ds = dscore_ref[s, wi]
            pb = probb_ref[s, wi]
            dq = dot(ds, kk, 0, 0)[0:64] * scale
            own_ds = jnp.concatenate([ds[0:64], ds[80:144]], axis=0)
            own_pb = jnp.concatenate([pb[0:64], pb[80:144]], axis=0)
            dk = dot(own_ds, q, 1, 0) * scale
            dv = dot(own_pb, c, 1, 0)
            dk = jnp.where(low_lanes, dk[0:64], dk[64:128])
            dv = jnp.where(low_lanes, dv[0:64], dv[64:128])
            rows = slice(4 * wi, 4 * wi + 4)
            dqs[rows, :, cols] = dq.astype(BF).reshape(4, 16, 128)
            dks[rows, :, cols] = dk.astype(BF).reshape(4, 16, 128)
            dvs[rows, :, cols] = dv.astype(BF).reshape(4, 16, 128)
        return carry

    lax.fori_loop(0, slabs // 2, gradients, 0)

    for a, b, c in xcs:
        arx(a, b, c, xl ^ a, xh ^ b, core ^ c, xl, xh, core).wait_recv()
    total = ax[0, 0] + ax[0, 1]
    for j in range(1, XL * XH):
        total = total + (ax[j, 0] + ax[j, 1])
    az[z] = total

    def arz(d, z_, zslot):
        return remote(
            az.at[zslot], az.at[zslot], arz_s.at[d], arz_r.at[d], at(xl, z_, xh, y, core)
        )

    arz_sent = [arz(d, z_, z) for d, z_, _ in zs]
    for copy in arz_sent:
        copy.start()

    lax.fori_loop(slabs // 2, slabs, gradients, 0)
    outs = [
        pltpu.make_async_copy(dqs.at[2:18], dq_out.at[0], out_sem.at[0]),
        pltpu.make_async_copy(dks.at[2:18], dk_out.at[0], out_sem.at[1]),
        pltpu.make_async_copy(dvs.at[2:18], dv_out.at[0], out_sem.at[2]),
    ]
    for copy in outs:
        copy.start()

    for d, z_, zsrc in zs:
        rsz(d, zsrc, zsrc).wait_recv()
    total = rz[0].astype(F32)
    for j in range(1, nz):
        total = total + rz[j].astype(F32)
    rsum[...] = total.astype(BF)

    def rsy(d, y_, slot):
        cols = pl.ds(pl.multiple_of((y_ // 2) * 128, 128), 128)
        return remote(
            rsum.at[:, cols], ry.at[slot], rsy_s.at[d], rsy_r.at[d], at(xl, z, xh, y_, core)
        )

    rsy_sent = [rsy(d, y_, y) for d, y_, _ in ys]
    for copy in rsy_sent:
        copy.start()
    ry[y] = rsum[:, pl.ds(pl.multiple_of((y // 2) * 128, 128), 128)]

    for d, _, zsrc in zs:
        arz(d, zsrc, zsrc).wait_recv()
    total = az[0]
    for j in range(1, nz):
        total = total + az[j]
    ay[y] = total

    def ary(d, y_, slot):
        return remote(ay.at[slot], ay.at[slot], ary_s.at[d], ary_r.at[d], at(xl, z, xh, y_, core))

    ary_sent = [ary(d, y_, y) for d, y_, _ in ys]
    for copy in ary_sent:
        copy.start()

    for d, _, ysrc in ys:
        rsy(d, ysrc, ysrc).wait_recv()
    total = ry[0].astype(F32)
    for j in range(1, ny):
        total = total + ry[j].astype(F32)
    fin[core] = total
    swap = remote(fin.at[core], fin.at[core], ag0_s.at[1], ag0_r.at[1], sibling)
    swap_got = remote(fin.at[1 - core], fin.at[1 - core], ag0_s.at[1], ag0_r.at[1], sibling)
    swap.start()

    for d, _, ysrc in ys:
        ary(d, ysrc, ysrc).wait_recv()
    total = ay[0]
    for j in range(1, ny):
        total = total + ay[j]
    back = lax.rem(128 - lane0, 128)
    bg_out[...] = total[0:heads, 0:49] * factor
    row = lax.broadcasted_iota(jnp.int32, (8, 128), 0)
    gate_sum = jnp.sum(jnp.where(row == y // 2, total[8:16], 0.0), axis=0, keepdims=True) * factor
    gate_sum = pltpu.roll(jnp.broadcast_to(gate_sum, (8, 128)), back, 1)
    tg_out[...] = (emb_mine[...] * gate_sum[0:1])[:, 0:32]

    swap_got.wait_recv()
    gate_mine = gate_ref[0:1, pl.ds(pl.multiple_of((lon // 4) * 128, 128), 128)]
    block = fin[...].reshape(32, 128) * gate_mine * factor
    wg_out[...] = pltpu.roll(block, back, 1)[:, 0:32]
    results = [(wg_out, wg_hbm), (tg_out, tg_hbm), (bg_out, bg_hbm)]
    results = [pltpu.make_async_copy(a, b, out_sem.at[3 + i]) for i, (a, b) in enumerate(results)]
    for copy in results:
        copy.start()

    sent = [ag0, swap] + lat_qkv + lon_qkv + late + agy_sent + agz_sent + agx_sent + rsx_sent
    sent += rsz_sent + rsy_sent + ary_sent + arz_sent + arx_sent
    sent += [agc(a, b) for a, b in [(0, 0)] + xs]
    for copy in sent:
        copy.wait_send()
    lax.fori_loop(0, slabs, lambda s, c: (rsc(s).wait_send(), c)[1], 0)
    for copy in outs + results:
        copy.wait()


def body(
    query_field, key_field, value_field, out_grad, out_weight, time_weight, rel_bias, timesteps
):
    frames, tile_rows, tile_cols, hd = query_field.shape
    model = out_grad.shape[3]
    heads = rel_bias.shape[0]
    nlat, nlon = lax.axis_size("lat"), lax.axis_size("lon")
    nz, ny = nlat // XL, nlon // (2 * XH)
    factor = 1.0 / math.sqrt(frames * tile_rows * nlat * tile_cols * nlon)
    half = model // XH
    slabs = hd // 128
    width = 3 * hd + model
    selq, selk = strip_tables()
    offs, foldk, foldq = place_tables()
    hbm = pl.BlockSpec(memory_space=pltpu.HBM)
    small_outs = [
        jax.ShapeDtypeStruct(out_weight.shape, F32),
        jax.ShapeDtypeStruct((time_weight.shape[0] // nlat, model // nlon), F32),
        jax.ShapeDtypeStruct(rel_bias.shape, F32),
    ]
    dma = pltpu.SemaphoreType.DMA
    field = jax.ShapeDtypeStruct(query_field.shape, BF)
    sems = [dma((12,)), dma((6,))]
    for shape in (
        (16,),
        (2,),
        (ny,),
        (nz,),
        (XL, XH),
        (XL, XH),
        (slabs,),
        (XL, XH),
        (nz,),
        (ny,),
        (ny,),
        (nz,),
        (XL, XH, 2),
    ):
        sems += [dma(shape), dma(shape)]
    out_shape = [field, field, field] + small_outs
    results = pl.pallas_call(
        functools.partial(kernel, nz, ny, hd, model, factor),
        out_shape=out_shape,
        in_specs=[hbm] * 12,
        out_specs=[hbm] * 6,
        scratch_shapes=[
            pltpu.VMEM(out_weight.shape, BF),
            pltpu.VMEM(time_weight.shape, BF),
            pltpu.SMEM(rel_bias.shape, F32),
            pltpu.SMEM((1, 1), jnp.int32),
            pltpu.VMEM((448, 256), F32),
            pltpu.VMEM((80, 80), jnp.int32),
            pltpu.VMEM((32, 160), F32),
            pltpu.VMEM((80, 16), F32),
            pltpu.VMEM((20, 16, width), BF),
            pltpu.VMEM((5, 16, width), BF),
            pltpu.VMEM((2, 7, 2, 16, hd), BF),
            pltpu.VMEM((2, 7, 2, 16, hd), BF),
            pltpu.VMEM((2, 7, 16, hd), BF),
            pltpu.VMEM((2, 7, 16, hd), BF),
            pltpu.VMEM((2, 16, 128), BF),
            pltpu.VMEM((16, 128), BF),
            pltpu.VMEM((ny, 16, 128), BF),
            pltpu.VMEM((nz, 16, half), BF),
            pltpu.VMEM((nlat, 2, 16, model), BF),
            pltpu.VMEM((5, 80, model), BF),
            pltpu.VMEM((8, model), F32),
            pltpu.VMEM((time_weight.shape[0] // nlat, 128), F32),
            pltpu.VMEM((heads, 80, 80), F32),
            pltpu.VMEM((slabs, 5, 160, 80), F32),
            pltpu.VMEM((slabs, 5, 160, 80), BF),
            pltpu.VMEM((slabs, 5, 160, 80), BF),
            pltpu.VMEM((slabs, 400, 128), BF),
            pltpu.VMEM((nlat, 2, 16, model), BF),
            pltpu.VMEM((nlat, 16, model), BF),
            pltpu.VMEM((nlat, 16, model), BF),
            pltpu.VMEM((XL * XH, nz, 16, half), BF),
            pltpu.VMEM((nz, 16, half), BF),
            pltpu.VMEM((nz, 16, half), BF),
            pltpu.VMEM((16, half), BF),
            pltpu.VMEM((ny, 16, 128), BF),
            pltpu.VMEM((2, 16, 128), F32),
            pltpu.VMEM((20, 16, hd), BF),
            pltpu.VMEM((20, 16, hd), BF),
            pltpu.VMEM((20, 16, hd), BF),
            pltpu.VMEM((16 * heads, 16), F32),
            pltpu.VMEM((XH, 16, 128), F32),
            pltpu.VMEM((XL * XH, 2, 16, 128), F32),
            pltpu.VMEM((nz, 16, 128), F32),
            pltpu.VMEM((ny, 16, 128), F32),
        ]
        + [pltpu.VMEM(o.shape, F32) for o in small_outs]
        + sems,
        compiler_params=pltpu.CompilerParams(
            collective_id=0, has_side_effects=True, vmem_limit_bytes=VMEM_LIMIT
        ),
        cost_estimate=pl.CostEstimate(
            flops=2_000_000_000, bytes_accessed=4_000_000, transcendentals=1_000_000
        ),
    )(
        query_field,
        key_field,
        value_field,
        out_grad,
        out_weight,
        time_weight,
        rel_bias,
        timesteps.reshape(1, 1),
        jnp.asarray(np.concatenate([selq, selk])),
        jnp.asarray(offs),
        jnp.asarray(foldk),
        jnp.asarray(foldq),
    )
    return pl.pallas_call(
        hand_out,
        out_shape=out_shape,
        in_specs=[hbm] * 6,
        out_specs=[hbm] * 6,
        scratch_shapes=[pltpu.VMEM(o.shape, o.dtype) for o in out_shape] + [dma((2, 6))],
        compiler_params=pltpu.CompilerParams(vmem_limit_bytes=VMEM_LIMIT),
    )(*results)


def hand_out(*refs):
    sem = refs[18]
    loads = [pltpu.make_async_copy(refs[i], refs[12 + i], sem.at[0, i]) for i in range(6)]
    stores = [pltpu.make_async_copy(refs[12 + i], refs[6 + i], sem.at[1, i]) for i in range(6)]
    for load in loads:
        load.start()
    for load, store in zip(loads, stores):
        load.wait()
        store.start()
    for store in stores:
        store.wait()


def solution(mesh):
    tile = P(None, "lat", "lon", None)
    return jax.shard_map(
        body,
        mesh=mesh,
        in_specs=(tile, tile, tile, tile, P("lat", "lon"), P(), P(), P()),
        out_specs=(tile, tile, tile, P("lat", "lon"), P("lat", "lon"), P()),
        check_vma=False,
    )
```

time: 85.1 us -> 59 us (0.69); the launches traced: 83.6 us -> 58.8 us
  local copies, waits for them, and re-layouts: 14.3 us -> 0 us
  Pallas kernels: 68 us -> 57.5 us
    unnamed x30 -> x0, local copies, waits for them, and re-layouts: 14.3 us -> none
    pallas_call x1, Pallas kernels: 68 us -> 55.6 us  [body(): pl.pallas_call(functools.partial(kernel, nz, ny, hd, model, factor), out_...]
    pallas_call x0 -> x1, Pallas kernels: none -> 1.94 us  [body(): pl.pallas_call(hand_out, out_shape=out_shape, in_specs=[hbm] * 6, out_spe...]
where the time goes in v2:
time: 59 us; the launch traced here: 58.8 us
  Pallas kernels  57.5 us (97%)
  between operations  1.29 us (2%)
    pallas_call x1, Pallas kernels, body(): pl.pallas_call(functools.partial(kernel, nz, ny, hd, model, factor), out_...  55.6 us
    pallas_call x1, Pallas kernels, body(): pl.pallas_call(hand_out, out_shape=out_shape, in_specs=[hbm] * 6, out_spe...  1.94 us

profile of v2, /device:TPU:1, one launch (start us, length us, event | category | flops | bytes accessed | tf_op | source)
XLA Modules:
  0.0 58.8 jit_solution(559405152738152027)
XLA Ops:
  1.3 55.6 %shard_map.163 = (bf16[1,16,16,512]{3,2,1,0:T(8,128)(2,1)}, bf16[1,16,16,512]{3,2,1,0:T(8,128)(2,1)}, bf16[1,16,16,512]{3,2,1,0:T(8,128)(2,1)}, f32[32,32]{1,0:T...) custom-call(bf16[1,16,16,512]{3,2,1,0:T(8,128)(2,1)} %q_in.1, bf16[1,16,16,512]{3,2,1,0:T(8,128)(2,1)} %k_in.1, ...), custom_call_target="tpu_custom_call" | custom-call | flops 2000000000 | bytes 4000000 | tf_op jit(solution)/shard_map/pallas_call | solution.py:771
  56.8 1.9 %shard_map.164 = (bf16[1,16,16,512]{3,2,1,0:T(8,128)(2,1)}, bf16[1,16,16,512]{3,2,1,0:T(8,128)(2,1)}, bf16[1,16,16,512]{3,2,1,0:T(8,128)(2,1)}, f32[32,32]{1,0:T...) custom-call(bf16[1,16,16,512]{3,2,1,0:T(8,128)(2,1)} %get-tuple-element.12.refs_0_, ...), custom_call_target="tpu_custom_call" | custom-call | tf_op jit(solution)/shard_map/pallas_call | solution.py:844

commit v3 on v2

--- a/solution.py
+++ b/solution.py
@@ -39,6 +39,15 @@
                     first[way, block, low if way == 0 else low + 8, token] = 1.0
                     second[way, block, low + 8 if way == 0 else low, token] = 1.0
     return first.reshape(224, 256), second.reshape(224, 256)
+
+
+def column_order():
+    order = np.zeros((256, 256), np.float32)
+    for row in range(4):
+        for core in range(2):
+            for j in range(32):
+                order[row * 64 + core * 32 + j, core * 128 + row * 32 + j] = 1.0
+    return order
 
 
 def slot_places(swap):
@@ -109,8 +118,6 @@
     rcv,
     snd2,
     rcv2,
-    slab,
-    slab_got,
     yb,
     wz,
     wf,
@@ -125,12 +132,12 @@
     mb,
     rc,
     mc,
-    rx,
+    rx1,
+    rx2,
     mz,
     rz,
     rsum,
     ry,
-    fin,
     dqs,
     dks,
     dvs,
@@ -146,8 +153,6 @@
     out_sem,
     halo_s,
     halo_r,
-    ag0_s,
-    ag0_r,
     agy_s,
     agy_r,
     agz_s,
@@ -176,20 +181,21 @@
     nlat, nlon = XL * nz, XH * ny * 2
     xl, z = lat // nz, lat % nz
     xh, y, core = lon // (2 * ny), (lon // 2) % ny, lon % 2
-    half = model // XH
+    half, quarter = model // 2, model // 4
     slabs = hd // 128
     heads = hd // 64
     width = 3 * hd + model
     og0 = 3 * hd
-    groups = ny // 2
+    groups = ny // 4
 
     def at(xl_, z_, xh_, y_, core_):
         return (xl_ * nz + z_, xh_ * 2 * ny + y_ * 2 + core_)
 
-    zs = [(d, lax.rem(z + d, nz), lax.rem(z - d + nz, nz)) for d in range(1, nz)]
-    xs = [(a, b) for a in range(XL) for b in range(XH) if a + b]
+    far_z = sorted(range(1, nz), key=lambda d: -min(d, nz - d))
+    far_y = sorted(range(1, ny), key=lambda d: -min(d, ny - d))
+    zs = [(d, lax.rem(z + d, nz), lax.rem(z - d + nz, nz)) for d in far_z]
     xcs = [(a, b, c) for a in range(XL) for b in range(XH) for c in range(2) if a + b + c]
-    ys = [(d, lax.rem(y + d, ny), lax.rem(y - d + ny, ny)) for d in range(1, ny)]
+    ys = [(d, lax.rem(y + d, ny), lax.rem(y - d + ny, ny)) for d in far_y]
     up, down = lax.rem(lat + nlat - 1, nlat), lax.rem(lat + 1, nlat)
     left, right = lax.rem(lon + nlon - 1, nlon), lax.rem(lon + 1, nlon)
 
@@ -205,12 +211,12 @@
 
     barrier = pltpu.get_barrier_semaphore()
     sibling = at(xl, z, xh, y, 1 - core)
-    peers = [sibling]
-    peers += [at(xl, z, xh, y_, core) for _, y_, _ in ys]
+    peers = [at(xl, z, xh, y_, core) for _, y_, _ in ys]
     peers += [at(xl, z_, xh, y, core) for _, z_, _ in zs]
     peers += [at(xl ^ a, z, xh ^ b, y, core ^ c) for a, b, c in xcs]
     peers += [(up, lon), (down, lon)]
     peers += [(i, j) for j in (left, right) for i in (lat, up, down)]
+    peers += [sibling]
     for peer in peers:
         pl.semaphore_signal(barrier, inc=1, device_id=peer, device_id_type=MESH)
 
@@ -234,15 +240,20 @@
 
     lane = lax.broadcasted_iota(jnp.int32, (32, 128), 1)
     row = lax.broadcasted_iota(jnp.int32, (32, 128), 0)
-    lane0 = lax.rem(lon, 4) * 32
+    lane0 = lax.rem(y, 4) * 32
     spread = (lane == row + lane0).astype(F32).astype(BF)
     loads[0].wait()
-    slab[...] = dot(w_in[...], spread, 1, 0).astype(BF).reshape(2, 16, 128)
+    yb[y] = dot(w_in[...], spread, 1, 0).astype(BF)
     pl.semaphore_wait(barrier, len(peers))
-    ag0 = remote(slab.at[1 - core], slab_got, ag0_s.at[0], ag0_r.at[0], sibling)
-    ag0.start()
-
-    for load in loads[1:5]:
+
+    def agy(d, y_, slot):
+        return remote(yb.at[slot], yb.at[slot], agy_s.at[d], agy_r.at[d], at(xl, z, xh, y_, core))
+
+    agy_sent = [agy(d, y_, y) for d, y_, _ in ys]
+    for copy in agy_sent:
+        copy.start()
+
+    for load in loads[1:4]:
         load.wait()
     lat_qkv = [
         remote(
@@ -255,17 +266,21 @@
     for copy in lat_qkv:
         copy.start()
 
-    ag0.wait_recv()
-    yb[y] = slab[core] + slab_got[...]
-
-    def agy(d, y_, slot):
-        return remote(yb.at[slot], yb.at[slot], agy_s.at[d], agy_r.at[d], at(xl, z, xh, y_, core))
-
-    agy_sent = [agy(d, y_, y) for d, y_, _ in ys]
-    for copy in agy_sent:
-        copy.start()
-
+    loads[4].wait()
     loads[5].wait()
+    order = sel[448:704].astype(BF)
+
+    def reorder(blocks):
+        moved = [dot(block, order, 1, 0).astype(BF) for block in blocks]
+        return [m[:, 0:128] for m in moved] + [m[:, 128:256] for m in moved]
+
+    og_blocks = [
+        xe[2:18, :, og0 + 256 * i : og0 + 256 * (i + 1)].reshape(256, 256)
+        for i in range(model // 256)
+    ]
+    for i, block in enumerate(reorder(og_blocks)):
+        xe[2:18, :, og0 + 128 * i : og0 + 128 * (i + 1)] = block.reshape(16, 16, 128)
+
     fields = [
         xe[2:18, :, 0:hd].reshape(256, hd),
         xe[2:18, :, hd : 2 * hd].reshape(256, hd),
@@ -304,6 +319,7 @@
     lon_qkv = strips(snd, rcv, 2)
     for copy in lon_qkv:
         copy.start()
+
     snd2[...] = dot(sq, fields[4], 1, 0).astype(BF).reshape(2, 7, 16, hd)
     late = [
         remote(
@@ -342,7 +358,9 @@
         emb_hi,
         jnp.where(emb_row == 1, emb_mid, jnp.where(emb_row == 2, emb_lo, 0.0)),
     ).astype(BF)
-    gate = jnp.sum(dot(parts, tw_in[...], 1, 0), axis=0, keepdims=True)
+    tw_blocks = [tw_in[:, 256 * i : 256 * (i + 1)] for i in range(model // 256)]
+    tw = jnp.concatenate(reorder(tw_blocks), axis=1)
+    gate = jnp.sum(dot(parts, tw, 1, 0), axis=0, keepdims=True)
     gate_ref[...] = jnp.broadcast_to(gate, (8, model))
     emb_rows = 2 * half_emb // nlat
     index = lat * emb_rows + lax.broadcasted_iota(jnp.int32, (emb_rows, 128), 0)
@@ -366,7 +384,8 @@
     for d, _, ysrc in ys:
         agy(d, ysrc, ysrc).wait_recv()
     for g in range(groups):
-        wz[z, :, g * 128 : (g + 1) * 128] = yb[2 * g] + yb[2 * g + 1]
+        pair = [yb[4 * g + i] + yb[4 * g + i + 1] for i in (0, 2)]
+        wz[z, :, g * 128 : (g + 1) * 128] = pair[0] + pair[1]
 
     def agz(d, z_, zslot):
         return remote(
@@ -445,68 +464,101 @@
             attn.append(dot(prob_b, vv, 0, 0)[0:64].astype(BF))
         attn = jnp.concatenate(attn, axis=0)[32:288]
         og = xe[2:18, :, og0:width].reshape(256, model)
-        term = dot(attn, og, 0, 0).astype(BF).reshape(4, 2, 16, model)
+        term = dot(attn, og, 0, 0).astype(BF).reshape(4, 32, model)
         mb[pl.ds(4 * s, 4)] = term
         rsc(s).start()
         return carry
 
     def rsc(s):
         rows = pl.ds(4 * s, 4)
-        return remote(mb.at[rows, 1 - core], rc.at[rows], rsc_s.at[s], rsc_r.at[s], sibling)
-
-    lax.fori_loop(0, slabs // 2, forward, 0)
+        cols = pl.ds(pl.multiple_of((1 - core) * half, 128), half)
+        return remote(mb.at[rows, :, cols], rc.at[rows], rsc_s.at[s], rsc_r.at[s], sibling)
+
+    ours, theirs = xl * (slabs // 2), (1 - xl) * (slabs // 2)
+    forward(ours, 0)
+    for i in range(1, slabs // 2):
+        forward(ours + i, 0)
 
     for d, _, zsrc in zs:
         agz(d, zsrc, zsrc).wait_recv()
-
-    def agx(a, b, xlslot, xhslot, xl_, xh_):
+    near = [(1, 0), (1, 1)]
+
+    def piece(xl_, xh_, core_, part=None):
+        first, count = (xl_ * nz, nz) if part is None else (xl_ * nz + part * (nz // 2), nz // 2)
+        return wf.at[pl.ds(first, count), :, pl.ds(core_ * half + xh_ * quarter, quarter)]
+
+    def neighbour(b):
+        return at(1 - xl, z, xh ^ b, y, core)
+
+    def agx(b, part, slot_xl, slot_xh):
+        rows = pl.ds(part * (nz // 2), nz // 2)
         return remote(
-            wz,
-            wf.at[pl.ds(xlslot * nz, nz), core, :, pl.ds(xhslot * half, half)],
-            agx_s.at[a, b],
-            agx_r.at[a, b],
-            at(xl_, z, xh_, y, core),
+            wz.at[rows],
+            piece(slot_xl, slot_xh, core, part),
+            agx_s.at[part, b],
+            agx_r.at[part, b],
+            neighbour(b),
         )
 
-    agx_sent = [agx(a, b, xl, xh, xl ^ a, xh ^ b) for a, b in xs]
+    agx_sent = [agx(b, 1 - b, xl, xh) for _, b in near]
+    agx_sent += [agx(b, b, xl, xh) for _, b in near]
     for copy in agx_sent:
         copy.start()
-    wf[pl.ds(xl * nz, nz), core, :, pl.ds(xh * half, half)] = wz[...]
-
-    def agc(a, b):
-        xl_, xh_ = xl ^ a, xh ^ b
-        piece = wf.at[pl.ds(xl_ * nz, nz), core, :, pl.ds(xh_ * half, half)]
-        return remote(piece, piece, agc_s.at[a, b], agc_r.at[a, b], sibling)
-
-    def agc_got(a, b):
-        piece = wf.at[pl.ds((xl ^ a) * nz, nz), 1 - core, :, pl.ds((xh ^ b) * half, half)]
-        return remote(piece, piece, agc_s.at[a, b], agc_r.at[a, b], sibling)
-
-    agc(0, 0).start()
-    lax.fori_loop(slabs // 2, slabs, forward, 0)
-
-    def core_sum(s, carry):
+    my_cols = pl.ds(pl.multiple_of(core * half + xh * quarter, 128), quarter)
+    wf[pl.ds(xl * nz, nz), :, my_cols] = wz[...]
+
+    def agc(i, xl_, xh_, core_, part=None):
+        block = piece(xl_, xh_, core_, part)
+        return remote(block, block, agc_s.at[i], agc_r.at[i], sibling)
+
+    agc_sent = [agc(0, xl, xh, core)]
+    agc_sent[0].start()
+
+    def core_sum(s):
         rsc(s).wait_recv()
         rows = pl.ds(4 * s, 4)
-        mc[rows] = (mb[rows, core].astype(F32) + rc[rows].astype(F32)).astype(BF)
-        return carry
-
-    lax.fori_loop(0, slabs, core_sum, 0)
-
-    def rsx(a, b, slot_xl, slot_xh):
-        xl_, xh_ = xl ^ a, xh ^ b
+        cols = pl.ds(pl.multiple_of(core * half, 128), half)
+        mc[rows] = (mb[rows, :, cols].astype(F32) + rc[rows].astype(F32)).astype(BF)
+
+    def rsx1(b, part, xl_, xh_):
+        rows = pl.ds(xl_ * nz + part * (nz // 2), nz // 2)
         return remote(
-            mc.at[pl.ds(xl_ * nz, nz), :, pl.ds(xh_ * half, half)],
-            rx.at[slot_xl * XH + slot_xh],
-            rsx_s.at[a, b],
-            rsx_r.at[a, b],
-            at(xl_, z, xh_, y, core),
+            mc.at[rows, :, pl.ds(pl.multiple_of(xh_ * quarter, 128), quarter)],
+            rx1.at[b],
+            rsx_s.at[0, b],
+            rsx_r.at[0, b],
+            neighbour(b),
         )
 
-    rsx_sent = [rsx(a, b, xl, xh) for a, b in xs]
+    def rsx2(b):
+        return remote(
+            mc.at[pl.ds((1 - xl) * nz, nz), :, pl.ds((xh ^ b) * quarter, quarter)],
+            rx2.at[b],
+            rsx_s.at[1, b],
+            rsx_r.at[1, b],
+            neighbour(b),
+        )
+
+    forward(theirs, 0)
+    for i in range(slabs // 2):
+        core_sum(ours + i)
+    rsx_sent = [rsx1(b, b, xl, 1 - xh) for _, b in near]
     for copy in rsx_sent:
         copy.start()
-    rx[xl * XH + xh] = mc[pl.ds(xl * nz, nz), :, pl.ds(xh * half, half)]
+    for i in range(1, slabs // 2):
+        forward(theirs + i, 0)
+
+    def relay(b, xl_, xh_):
+        block = piece(xl_, xh_, core, b)
+        return remote(block, block, agx_s.at[2, b], agx_r.at[2, b], neighbour(b))
+
+    for _, b in near:
+        agx(b, 1 - b, 1 - xl, xh ^ b).wait_recv()
+    relays = [relay(b, 1 - xl, xh ^ b ^ 1) for _, b in near]
+    for copy in relays:
+        copy.start()
+    for i in range(slabs // 2):
+        core_sum(theirs + i)
 
     for copy in late:
         copy.wait_recv()
@@ -522,11 +574,10 @@
         ge[wi, 0:64] = (own.astype(F32) * gate_row).astype(BF)
         ge[wi, 64:80] = (lrx[wi, :, og0:width].astype(F32) * gate_row).astype(BF)
 
-    for a, b in xs:
-        agx(a, b, xl ^ a, xh ^ b, xl ^ a, xh ^ b).wait_recv()
-        agc(a, b).start()
-    for a, b in [(0, 0)] + xs:
-        agc_got(a, b).wait_recv()
+    for _, b in near:
+        agx(b, b, 1 - xl, xh ^ b).wait_recv()
+        agc_sent.append(agc(1 + b, 1 - xl, xh ^ b, core))
+        agc_sent[-1].start()
 
     def backward(s, gate_terms):
         weight = wf[pl.ds(4 * s, 4)].reshape(128, model)
@@ -558,7 +609,31 @@
         high = b.astype(BF)
         return dot(a, high, 1, 0) + dot(a, (b - high.astype(F32)).astype(BF), 1, 0)
 
-    gate_terms = lax.fori_loop(0, slabs, backward, jnp.zeros((8, model), F32))
+    for _, b in near:
+        agc(1 + b, 1 - xl, xh ^ b, 1 - core).wait_recv()
+    gate_terms = backward(theirs, jnp.zeros((8, model), F32))
+
+    for _, b in near:
+        relay(b, xl, 1 - xh).wait_recv()
+        agc_sent.append(agc(3 + b, xl, 1 - xh, core, b))
+        agc_sent[-1].start()
+
+    for _, b in near:
+        rsx1(b, b, xl, 1 - xh).wait_recv()
+        rows = pl.ds((1 - xl) * nz + b * (nz // 2), nz // 2)
+        cols = pl.ds(pl.multiple_of((xh ^ b ^ 1) * quarter, 128), quarter)
+        mc[rows, :, cols] = (mc[rows, :, cols].astype(F32) + rx1[b].astype(F32)).astype(BF)
+    second = [rsx2(b) for _, b in near]
+    for copy in second:
+        copy.start()
+    rsx_sent += second
+
+    for i in range(1, slabs // 2):
+        gate_terms = backward(theirs + i, gate_terms)
+    agc(0, xl, xh, 1 - core).wait_recv()
+    for _, b in near:
+        agc(3 + b, xl, 1 - xh, 1 - core, b).wait_recv()
+    gate_terms = lax.fori_loop(ours, ours + slabs // 2, backward, gate_terms)
     gate_terms = jnp.sum(gate_terms, axis=0, keepdims=True)
 
     term_row = lax.broadcasted_iota(jnp.int32, (16 * heads, 128), 0)
@@ -571,15 +646,22 @@
     by_offset = jnp.sum(by_offset.reshape(heads, 16, 128), axis=1)
     if heads < 8:
         by_offset = jnp.concatenate([by_offset, jnp.zeros((8 - heads, 128), F32)], axis=0)
-    for h in range(XH):
-        pay[h, 0:8] = by_offset
-        for g in range(8):
-            first = h * half + min(g, groups - 1) * 128
-            pay[h, 8 + g : 9 + g] = gate_terms[:, first : first + 128]
+    row = lax.broadcasted_iota(jnp.int32, (8, 128), 0)
+    upper = lax.broadcasted_iota(jnp.int32, (8, 128), 1) >= 64
+    for c in range(2):
+        for h in range(XH):
+            packed = by_offset
+            for i in range(quarter // 64):
+                first = c * half + h * quarter + (i // 2) * 128
+                lanes_i = jnp.broadcast_to(gate_terms[:, first : first + 128], (8, 128))
+                if i % 2 == 0:
+                    lanes_i = pltpu.roll(lanes_i, 64, 1)
+                packed = jnp.where(upper & (row == i), lanes_i, packed)
+            pay[c, h] = packed
 
     def arx(a, b, c, slot_xl, slot_xh, slot_core, xl_, xh_, core_):
         return remote(
-            pay.at[xh_],
+            pay.at[core_, xh_],
             ax.at[slot_xl * XH + slot_xh, slot_core],
             arx_s.at[a, b, c],
             arx_r.at[a, b, c],
@@ -589,15 +671,13 @@
     arx_sent = [arx(a, b, c, xl, xh, core, xl ^ a, xh ^ b, core ^ c) for a, b, c in xcs]
     for copy in arx_sent:
         copy.start()
-    ax[xl * XH + xh, core] = pay[xh]
-
-    for a, b in xs:
-        rsx(a, b, xl ^ a, xh ^ b).wait_recv()
+    ax[xl * XH + xh, core] = pay[core, xh]
+
+    for _, b in near:
+        rsx2(b).wait_recv()
     for i in range(nz):
-        total = rx[0, i].astype(F32)
-        for j in range(1, XL * XH):
-            total = total + rx[j, i].astype(F32)
-        mz[i] = total.astype(BF)
+        total = mc[xl * nz + i, :, pl.ds(pl.multiple_of(xh * quarter, 128), quarter)].astype(F32)
+        mz[i] = (total + rx2[0, i].astype(F32) + rx2[1, i].astype(F32)).astype(BF)
 
     def rsz(d, z_, zslot):
         return remote(mz.at[z_], rz.at[zslot], rsz_s.at[d], rsz_r.at[d], at(xl, z_, xh, y, core))
@@ -663,7 +743,7 @@
     rsum[...] = total.astype(BF)
 
     def rsy(d, y_, slot):
-        cols = pl.ds(pl.multiple_of((y_ // 2) * 128, 128), 128)
+        cols = pl.ds(pl.multiple_of((y_ // 4) * 128, 128), 128)
         return remote(
             rsum.at[:, cols], ry.at[slot], rsy_s.at[d], rsy_r.at[d], at(xl, z, xh, y_, core)
         )
@@ -671,7 +751,7 @@
     rsy_sent = [rsy(d, y_, y) for d, y_, _ in ys]
     for copy in rsy_sent:
         copy.start()
-    ry[y] = rsum[:, pl.ds(pl.multiple_of((y // 2) * 128, 128), 128)]
+    ry[y] = rsum[:, pl.ds(pl.multiple_of((y // 4) * 128, 128), 128)]
 
     for d, _, zsrc in zs:
         arz(d, zsrc, zsrc).wait_recv()
@@ -692,35 +772,29 @@
     total = ry[0].astype(F32)
     for j in range(1, ny):
         total = total + ry[j].astype(F32)
-    fin[core] = total
-    swap = remote(fin.at[core], fin.at[core], ag0_s.at[1], ag0_r.at[1], sibling)
-    swap_got = remote(fin.at[1 - core], fin.at[1 - core], ag0_s.at[1], ag0_r.at[1], sibling)
-    swap.start()
+    back = lax.rem(128 - lane0, 128)
+    first = core * half + xh * quarter + (y // 4) * 128
+    gate_mine = gate_ref[0:1, pl.ds(pl.multiple_of(first, 128), 128)]
+    wg_out[...] = pltpu.roll(total * gate_mine * factor, back, 1)[:, 0:32]
 
     for d, _, ysrc in ys:
         ary(d, ysrc, ysrc).wait_recv()
     total = ay[0]
     for j in range(1, ny):
         total = total + ay[j]
-    back = lax.rem(128 - lane0, 128)
     bg_out[...] = total[0:heads, 0:49] * factor
-    row = lax.broadcasted_iota(jnp.int32, (8, 128), 0)
-    gate_sum = jnp.sum(jnp.where(row == y // 2, total[8:16], 0.0), axis=0, keepdims=True) * factor
-    gate_sum = pltpu.roll(jnp.broadcast_to(gate_sum, (8, 128)), back, 1)
+    gate_sum = jnp.sum(jnp.where(row == y // 2, total, 0.0), axis=0, keepdims=True) * factor
+    gate_sum = pltpu.roll(jnp.broadcast_to(gate_sum, (8, 128)), 64 - lax.rem(y, 2) * 32, 1)
     tg_out[...] = (emb_mine[...] * gate_sum[0:1])[:, 0:32]
 
-    swap_got.wait_recv()
-    gate_mine = gate_ref[0:1, pl.ds(pl.multiple_of((lon // 4) * 128, 128), 128)]
-    block = fin[...].reshape(32, 128) * gate_mine * factor
-    wg_out[...] = pltpu.roll(block, back, 1)[:, 0:32]
     results = [(wg_out, wg_hbm), (tg_out, tg_hbm), (bg_out, bg_hbm)]
     results = [pltpu.make_async_copy(a, b, out_sem.at[3 + i]) for i, (a, b) in enumerate(results)]
     for copy in results:
         copy.start()
 
-    sent = [ag0, swap] + lat_qkv + lon_qkv + late + agy_sent + agz_sent + agx_sent + rsx_sent
+    sent = lat_qkv + lon_qkv + late + agy_sent + agz_sent + agx_sent + rsx_sent
     sent += rsz_sent + rsy_sent + ary_sent + arz_sent + arx_sent
-    sent += [agc(a, b) for a, b in [(0, 0)] + xs]
+    sent += relays + agc_sent
     for copy in sent:
         copy.wait_send()
     lax.fori_loop(0, slabs, lambda s, c: (rsc(s).wait_send(), c)[1], 0)
@@ -737,10 +811,11 @@
     nlat, nlon = lax.axis_size("lat"), lax.axis_size("lon")
     nz, ny = nlat // XL, nlon // (2 * XH)
     factor = 1.0 / math.sqrt(frames * tile_rows * nlat * tile_cols * nlon)
-    half = model // XH
+    half, quarter = model // 2, model // 4
     slabs = hd // 128
     width = 3 * hd + model
     selq, selk = strip_tables()
+    order = column_order()
     offs, foldk, foldq = place_tables()
     hbm = pl.BlockSpec(memory_space=pltpu.HBM)
     small_outs = [
@@ -753,13 +828,12 @@
     sems = [dma((12,)), dma((6,))]
     for shape in (
         (16,),
-        (2,),
         (ny,),
         (nz,),
-        (XL, XH),
-        (XL, XH),
+        (3, 2),
+        (5,),
         (slabs,),
-        (XL, XH),
+        (2, 2),
         (nz,),
         (ny,),
         (ny,),
@@ -778,7 +852,7 @@
             pltpu.VMEM(time_weight.shape, BF),
             pltpu.SMEM(rel_bias.shape, F32),
             pltpu.SMEM((1, 1), jnp.int32),
-            pltpu.VMEM((448, 256), F32),
+            pltpu.VMEM((704, 256), F32),
             pltpu.VMEM((80, 80), jnp.int32),
             pltpu.VMEM((32, 160), F32),
             pltpu.VMEM((80, 16), F32),
@@ -788,11 +862,9 @@
             pltpu.VMEM((2, 7, 2, 16, hd), BF),
             pltpu.VMEM((2, 7, 16, hd), BF),
             pltpu.VMEM((2, 7, 16, hd), BF),
-            pltpu.VMEM((2, 16, 128), BF),
-            pltpu.VMEM((16, 128), BF),
-            pltpu.VMEM((ny, 16, 128), BF),
-            pltpu.VMEM((nz, 16, half), BF),
-            pltpu.VMEM((nlat, 2, 16, model), BF),
+            pltpu.VMEM((ny, 32, 128), BF),
+            pltpu.VMEM((nz, 32, quarter), BF),
+            pltpu.VMEM((nlat, 32, model), BF),
             pltpu.VMEM((5, 80, model), BF),
             pltpu.VMEM((8, model), F32),
             pltpu.VMEM((time_weight.shape[0] // nlat, 128), F32),
@@ -801,23 +873,23 @@
             pltpu.VMEM((slabs, 5, 160, 80), BF),
             pltpu.VMEM((slabs, 5, 160, 80), BF),
             pltpu.VMEM((slabs, 400, 128), BF),
-            pltpu.VMEM((nlat, 2, 16, model), BF),
-            pltpu.VMEM((nlat, 16, model), BF),
-            pltpu.VMEM((nlat, 16, model), BF),
-            pltpu.VMEM((XL * XH, nz, 16, half), BF),
-            pltpu.VMEM((nz, 16, half), BF),
-            pltpu.VMEM((nz, 16, half), BF),
-            pltpu.VMEM((16, half), BF),
-            pltpu.VMEM((ny, 16, 128), BF),
-            pltpu.VMEM((2, 16, 128), F32),
+            pltpu.VMEM((nlat, 32, model), BF),
+            pltpu.VMEM((nlat, 32, half), BF),
+            pltpu.VMEM((nlat, 32, half), BF),
+            pltpu.VMEM((2, nz // 2, 32, quarter), BF),
+            pltpu.VMEM((2, nz, 32, quarter), BF),
+            pltpu.VMEM((nz, 32, quarter), BF),
+            pltpu.VMEM((nz, 32, quarter), BF),
+            pltpu.VMEM((32, quarter), BF),
+            pltpu.VMEM((ny, 32, 128), BF),
             pltpu.VMEM((20, 16, hd), BF),
             pltpu.VMEM((20, 16, hd), BF),
             pltpu.VMEM((20, 16, hd), BF),
             pltpu.VMEM((16 * heads, 16), F32),
-            pltpu.VMEM((XH, 16, 128), F32),
-            pltpu.VMEM((XL * XH, 2, 16, 128), F32),
-            pltpu.VMEM((nz, 16, 128), F32),
-            pltpu.VMEM((ny, 16, 128), F32),
+            pltpu.VMEM((2, XH, 8, 128), F32),
+            pltpu.VMEM((XL * XH, 2, 8, 128), F32),
+            pltpu.VMEM((nz, 8, 128), F32),
+            pltpu.VMEM((ny, 8, 128), F32),
         ]
         + [pltpu.VMEM(o.shape, F32) for o in small_outs]
         + sems,
@@ -836,7 +908,7 @@
         time_weight,
         rel_bias,
         timesteps.reshape(1, 1),
-        jnp.asarray(np.concatenate([selq, selk])),
+        jnp.asarray(np.concatenate([selq, selk, order])),
         jnp.asarray(offs),
         jnp.asarray(foldk),
         jnp.asarray(foldq),

time: 59 us -> 55.2 us (0.936)
  Pallas kernels: 57.5 us -> 53.7 us
    pallas_call x1, Pallas kernels: 55.6 us -> 51.8 us  [body(): pl.pallas_call(functools.partial(kernel, nz, ny, hd, model, factor), out_...]
where the time goes in v3:
time: 55.2 us; the launch traced here: 55 us
  Pallas kernels  53.7 us (97%)
  between operations  1.29 us (2%)
    pallas_call x1, Pallas kernels, body(): pl.pallas_call(functools.partial(kernel, nz, ny, hd, model, factor), out_...  51.8 us
    pallas_call x1, Pallas kernels, body(): pl.pallas_call(hand_out, out_shape=out_shape, in_specs=[hbm] * 6, out_spe...  1.94 us

profile of v3, /device:TPU:1, one launch (start us, length us, event | category | flops | bytes accessed | tf_op | source)
XLA Modules:
  0.0 55.0 jit_solution(2504501419363750553)
XLA Ops:
  1.3 51.8 %shard_map.163 = (bf16[1,16,16,512]{3,2,1,0:T(8,128)(2,1)}, bf16[1,16,16,512]{3,2,1,0:T(8,128)(2,1)}, bf16[1,16,16,512]{3,2,1,0:T(8,128)(2,1)}, f32[32,32]{1,0:T...) custom-call(bf16[1,16,16,512]{3,2,1,0:T(8,128)(2,1)} %q_in.1, bf16[1,16,16,512]{3,2,1,0:T(8,128)(2,1)} %k_in.1, ...), custom_call_target="tpu_custom_call" | custom-call | flops 2000000000 | bytes 4000000 | tf_op jit(solution)/shard_map/pallas_call | solution.py:845
  53.1 1.9 %shard_map.164 = (bf16[1,16,16,512]{3,2,1,0:T(8,128)(2,1)}, bf16[1,16,16,512]{3,2,1,0:T(8,128)(2,1)}, bf16[1,16,16,512]{3,2,1,0:T(8,128)(2,1)}, f32[32,32]{1,0:T...) custom-call(bf16[1,16,16,512]{3,2,1,0:T(8,128)(2,1)} %get-tuple-element.12.refs_0_, ...), custom_call_target="tpu_custom_call" | custom-call | tf_op jit(solution)/shard_map/pallas_call | solution.py:916

commit v4 on v3

--- a/solution.py
+++ b/solution.py
@@ -132,8 +132,10 @@
     mb,
     rc,
     mc,
-    rx1,
     rx2,
+    rd,
+    dsum,
+    dgot,
     mz,
     rz,
     rsum,
@@ -161,10 +163,14 @@
     agx_r,
     agc_s,
     agc_r,
+    agd_s,
+    agd_r,
     rsc_s,
     rsc_r,
     rsx_s,
     rsx_r,
+    rsd_s,
+    rsd_r,
     rsz_s,
     rsz_r,
     rsy_s,
@@ -392,9 +398,60 @@
             wz.at[zslot], wz.at[zslot], agz_s.at[d], agz_r.at[d], at(xl, z_, xh, y, core)
         )
 
+    near = [(1, 0), (1, 1)]
+
+    def columns(core_, xh_):
+        return pl.ds(pl.multiple_of(core_ * half + xh_ * quarter, 128), quarter)
+
+    def piece(xl_, xh_, core_):
+        return wf.at[pl.ds(xl_ * nz, nz), :, columns(core_, xh_)]
+
+    def neighbour(b):
+        return at(1 - xl, z, xh ^ b, y, core)
+
+    def agx(b, slot_xl, slot_xh):
+        return remote(
+            wz, piece(slot_xl, slot_xh, core), agx_s.at[b], agx_r.at[b], neighbour(b)
+        )
+
+    agx_sent = [agx(b, xl, xh) for _, b in near]
+
+    far = at(xl, z, 1 - xh, y, core)
+
+    def agf(xh_):
+        block = wf.at[xl * nz + z, :, columns(core, xh_)]
+        return remote(wz.at[z], block, agx_s.at[2], agx_r.at[2], far)
+
+    def agd(d, z_, zslot):
+        block = wf.at[xl * nz + zslot, :, columns(core, 1 - xh)]
+        return remote(block, block, agd_s.at[d], agd_r.at[d], at(xl, z_, xh, y, core))
+
+    agf_sent = agf(xh)
+    agf_sent.start()
     agz_sent = [agz(d, z_, z) for d, z_, _ in zs]
     for copy in agz_sent:
         copy.start()
+
+    def agc(i, xl_, xh_, core_):
+        block = piece(xl_, xh_, core_)
+        return remote(block, block, agc_s.at[i], agc_r.at[i], sibling)
+
+    agc_sent = [agc(0, xl, xh, core)]
+
+    def spread_x():
+        for d, _, zsrc in zs:
+            agz(d, zsrc, zsrc).wait_recv()
+        for copy in agx_sent:
+            copy.start()
+        wf[pl.ds(xl * nz, nz), :, columns(core, xh)] = wz[...]
+        agc_sent[0].start()
+
+
+    edge = (y == 0) | (y == ny - 1)
+
+    @pl.when(edge)
+    def _():
+        spread_x()
 
     for copy in lat_qkv + lon_qkv:
         copy.wait_recv()
@@ -476,43 +533,16 @@
 
     ours, theirs = xl * (slabs // 2), (1 - xl) * (slabs // 2)
     forward(ours, 0)
+    agf(1 - xh).wait_recv()
+    agd_sent = [agd(d, z_, z) for d, z_, _ in zs]
+    for copy in agd_sent:
+        copy.start()
     for i in range(1, slabs // 2):
         forward(ours + i, 0)
 
-    for d, _, zsrc in zs:
-        agz(d, zsrc, zsrc).wait_recv()
-    near = [(1, 0), (1, 1)]
-
-    def piece(xl_, xh_, core_, part=None):
-        first, count = (xl_ * nz, nz) if part is None else (xl_ * nz + part * (nz // 2), nz // 2)
-        return wf.at[pl.ds(first, count), :, pl.ds(core_ * half + xh_ * quarter, quarter)]
-
-    def neighbour(b):
-        return at(1 - xl, z, xh ^ b, y, core)
-
-    def agx(b, part, slot_xl, slot_xh):
-        rows = pl.ds(part * (nz // 2), nz // 2)
-        return remote(
-            wz.at[rows],
-            piece(slot_xl, slot_xh, core, part),
-            agx_s.at[part, b],
-            agx_r.at[part, b],
-            neighbour(b),
-        )
-
-    agx_sent = [agx(b, 1 - b, xl, xh) for _, b in near]
-    agx_sent += [agx(b, b, xl, xh) for _, b in near]
-    for copy in agx_sent:
-        copy.start()
-    my_cols = pl.ds(pl.multiple_of(core * half + xh * quarter, 128), quarter)
-    wf[pl.ds(xl * nz, nz), :, my_cols] = wz[...]
-
-    def agc(i, xl_, xh_, core_, part=None):
-        block = piece(xl_, xh_, core_, part)
-        return remote(block, block, agc_s.at[i], agc_r.at[i], sibling)
-
-    agc_sent = [agc(0, xl, xh, core)]
-    agc_sent[0].start()
+    @pl.when(jnp.logical_not(edge))
+    def _():
+        spread_x()
 
     def core_sum(s):
         rsc(s).wait_recv()
@@ -520,45 +550,48 @@
         cols = pl.ds(pl.multiple_of(core * half, 128), half)
         mc[rows] = (mb[rows, :, cols].astype(F32) + rc[rows].astype(F32)).astype(BF)
 
-    def rsx1(b, part, xl_, xh_):
-        rows = pl.ds(xl_ * nz + part * (nz // 2), nz // 2)
+    far_cols = pl.ds(pl.multiple_of((1 - xh) * quarter, 128), quarter)
+
+    def rsd(d, z_, zslot):
         return remote(
-            mc.at[rows, :, pl.ds(pl.multiple_of(xh_ * quarter, 128), quarter)],
-            rx1.at[b],
-            rsx_s.at[0, b],
-            rsx_r.at[0, b],
-            neighbour(b),
+            mc.at[xl * nz + z_, :, far_cols],
+            rd.at[zslot],
+            rsd_s.at[d],
+            rsd_r.at[d],
+            at(xl, z_, xh, y, core),
         )
+
+    far_sum = remote(dsum, dgot, rsx_s.at[2], rsx_r.at[2], far)
 
     def rsx2(b):
         return remote(
             mc.at[pl.ds((1 - xl) * nz, nz), :, pl.ds((xh ^ b) * quarter, quarter)],
             rx2.at[b],
-            rsx_s.at[1, b],
-            rsx_r.at[1, b],
+            rsx_s.at[b],
+            rsx_r.at[b],
             neighbour(b),
         )
 
     forward(theirs, 0)
     for i in range(slabs // 2):
         core_sum(ours + i)
-    rsx_sent = [rsx1(b, b, xl, 1 - xh) for _, b in near]
-    for copy in rsx_sent:
-        copy.start()
+    rsd_sent = [rsd(d, z_, z) for d, z_, _ in zs]
+    for copy in rsd_sent:
+        copy.start()
+    rd[z] = mc[xl * nz + z, :, far_cols]
     for i in range(1, slabs // 2):
         forward(theirs + i, 0)
 
-    def relay(b, xl_, xh_):
-        block = piece(xl_, xh_, core, b)
-        return remote(block, block, agx_s.at[2, b], agx_r.at[2, b], neighbour(b))
-
     for _, b in near:
-        agx(b, 1 - b, 1 - xl, xh ^ b).wait_recv()
-    relays = [relay(b, 1 - xl, xh ^ b ^ 1) for _, b in near]
-    for copy in relays:
-        copy.start()
+        agx(b, 1 - xl, xh ^ b).wait_recv()
+        agc_sent.append(agc(1 + b, 1 - xl, xh ^ b, core))
+        agc_sent[-1].start()
+
     for i in range(slabs // 2):
         core_sum(theirs + i)
+    rsx_sent = [rsx2(b) for _, b in near]
+    for copy in rsx_sent:
+        copy.start()
 
     for copy in late:
         copy.wait_recv()
@@ -574,20 +607,19 @@
         ge[wi, 0:64] = (own.astype(F32) * gate_row).astype(BF)
         ge[wi, 64:80] = (lrx[wi, :, og0:width].astype(F32) * gate_row).astype(BF)
 
-    for _, b in near:
-        agx(b, b, 1 - xl, xh ^ b).wait_recv()
-        agc_sent.append(agc(1 + b, 1 - xl, xh ^ b, core))
-        agc_sent[-1].start()
+    def cotangent(s):
+        weight = wf[pl.ds(4 * s, 2 * slabs)].reshape(64 * slabs, model)
+        cot = dot(ge[...].reshape(400, model), weight, 1, 1).astype(BF)
+        for i in range(slabs // 2):
+            cot_ref[s + i] = cot[:, 128 * i : 128 * (i + 1)]
 
     def backward(s, gate_terms):
         weight = wf[pl.ds(4 * s, 4)].reshape(128, model)
-        cot = dot(ge[...].reshape(400, model), weight, 1, 1).astype(BF)
-        cot_ref[s] = cot
         bias_sum = jnp.zeros((160, 80), F32)
         for wi in range(5):
             vv = both(group(wi, 2 * hd, s))
             prob = prob_ref[s, wi].reshape(2, 80, 80)
-            dprob = dot(vv, cot[80 * wi : 80 * wi + 80], 1, 1).reshape(2, 80, 80)
+            dprob = dot(vv, cot_ref[s, 80 * wi : 80 * wi + 80], 1, 1).reshape(2, 80, 80)
             inner = jnp.sum(prob * dprob, axis=1, keepdims=True)
             dscore = (prob * (dprob - inner)).reshape(160, 80)
             if wi in (0, 4):
@@ -611,28 +643,26 @@
 
     for _, b in near:
         agc(1 + b, 1 - xl, xh ^ b, 1 - core).wait_recv()
+    cotangent(theirs)
     gate_terms = backward(theirs, jnp.zeros((8, model), F32))
 
-    for _, b in near:
-        relay(b, xl, 1 - xh).wait_recv()
-        agc_sent.append(agc(3 + b, xl, 1 - xh, core, b))
-        agc_sent[-1].start()
-
-    for _, b in near:
-        rsx1(b, b, xl, 1 - xh).wait_recv()
-        rows = pl.ds((1 - xl) * nz + b * (nz // 2), nz // 2)
-        cols = pl.ds(pl.multiple_of((xh ^ b ^ 1) * quarter, 128), quarter)
-        mc[rows, :, cols] = (mc[rows, :, cols].astype(F32) + rx1[b].astype(F32)).astype(BF)
-    second = [rsx2(b) for _, b in near]
-    for copy in second:
-        copy.start()
-    rsx_sent += second
-
+    for d, _, zsrc in zs:
+        agd(d, zsrc, zsrc).wait_recv()
+    agc_sent.append(agc(3, xl, 1 - xh, core))
+    agc_sent[-1].start()
     for i in range(1, slabs // 2):
         gate_terms = backward(theirs + i, gate_terms)
+
+    for d, _, zsrc in zs:
+        rsd(d, zsrc, zsrc).wait_recv()
+    total = rd[0].astype(F32)
+    for j in range(1, nz):
+        total = total + rd[j].astype(F32)
+    dsum[...] = total.astype(BF)
+    far_sum.start()
     agc(0, xl, xh, 1 - core).wait_recv()
-    for _, b in near:
-        agc(3 + b, xl, 1 - xh, 1 - core, b).wait_recv()
+    agc(3, xl, 1 - xh, 1 - core).wait_recv()
+    cotangent(ours)
     gate_terms = lax.fori_loop(ours, ours + slabs // 2, backward, gate_terms)
     gate_terms = jnp.sum(gate_terms, axis=0, keepdims=True)
 
@@ -737,8 +767,9 @@
 
     for d, z_, zsrc in zs:
         rsz(d, zsrc, zsrc).wait_recv()
-    total = rz[0].astype(F32)
-    for j in range(1, nz):
+    far_sum.wait_recv()
+    total = dgot[...].astype(F32)
+    for j in range(nz):
         total = total + rz[j].astype(F32)
     rsum[...] = total.astype(BF)
 
@@ -794,7 +825,7 @@
 
     sent = lat_qkv + lon_qkv + late + agy_sent + agz_sent + agx_sent + rsx_sent
     sent += rsz_sent + rsy_sent + ary_sent + arz_sent + arx_sent
-    sent += relays + agc_sent
+    sent += agc_sent + agd_sent + rsd_sent + [agf_sent, far_sum]
     for copy in sent:
         copy.wait_send()
     lax.fori_loop(0, slabs, lambda s, c: (rsc(s).wait_send(), c)[1], 0)
@@ -830,10 +861,12 @@
         (16,),
         (ny,),
         (nz,),
-        (3, 2),
-        (5,),
+        (3,),
+        (4,),
+        (nz,),
         (slabs,),
-        (2, 2),
+        (3,),
+        (nz,),
         (nz,),
         (ny,),
         (ny,),
@@ -876,8 +909,10 @@
             pltpu.VMEM((nlat, 32, model), BF),
             pltpu.VMEM((nlat, 32, half), BF),
             pltpu.VMEM((nlat, 32, half), BF),
-            pltpu.VMEM((2, nz // 2, 32, quarter), BF),
             pltpu.VMEM((2, nz, 32, quarter), BF),
+            pltpu.VMEM((nz, 32, quarter), BF),
+            pltpu.VMEM((32, quarter), BF),
+            pltpu.VMEM((32, quarter), BF),
             pltpu.VMEM((nz, 32, quarter), BF),
             pltpu.VMEM((nz, 32, quarter), BF),
             pltpu.VMEM((32, quarter), BF),

time: 55.2 us -> 54.9 us (level)
  no operation moved by 1% of the time
where the time goes in v4:
time: 54.9 us; the launch traced here: 54.7 us
  Pallas kernels  53.4 us (97%)
  between operations  1.29 us (2%)
    pallas_call x1, Pallas kernels, body(): pl.pallas_call(functools.partial(kernel, nz, ny, hd, model, factor), out_...  51.5 us
    pallas_call x1, Pallas kernels, body(): pl.pallas_call(hand_out, out_shape=out_shape, in_specs=[hbm] * 6, out_spe...  1.94 us

profile of v4, /device:TPU:1, one launch (start us, length us, event | category | flops | bytes accessed | tf_op | source)
XLA Modules:
  0.0 54.7 jit_solution(15268038288546472515)
XLA Ops:
  1.3 51.5 %shard_map.163 = (bf16[1,16,16,512]{3,2,1,0:T(8,128)(2,1)}, bf16[1,16,16,512]{3,2,1,0:T(8,128)(2,1)}, bf16[1,16,16,512]{3,2,1,0:T(8,128)(2,1)}, f32[32,32]{1,0:T...) custom-call(bf16[1,16,16,512]{3,2,1,0:T(8,128)(2,1)} %q_in.1, bf16[1,16,16,512]{3,2,1,0:T(8,128)(2,1)} %k_in.1, ...), custom_call_target="tpu_custom_call" | custom-call | flops 2000000000 | bytes 4000000 | tf_op jit(solution)/shard_map/pallas_call | solution.py:878
  52.8 1.9 %shard_map.164 = (bf16[1,16,16,512]{3,2,1,0:T(8,128)(2,1)}, bf16[1,16,16,512]{3,2,1,0:T(8,128)(2,1)}, bf16[1,16,16,512]{3,2,1,0:T(8,128)(2,1)}, f32[32,32]{1,0:T...) custom-call(bf16[1,16,16,512]{3,2,1,0:T(8,128)(2,1)} %get-tuple-element.12.refs_0_, ...), custom_call_target="tpu_custom_call" | custom-call | tf_op jit(solution)/shard_map/pallas_call | solution.py:951

commit v5 on v4

--- a/solution.py
+++ b/solution.py
@@ -533,16 +533,17 @@
 
     ours, theirs = xl * (slabs // 2), (1 - xl) * (slabs // 2)
     forward(ours, 0)
+    for i in range(1, slabs // 2):
+        forward(ours + i, 0)
+
+    @pl.when(jnp.logical_not(edge))
+    def _():
+        spread_x()
+
     agf(1 - xh).wait_recv()
     agd_sent = [agd(d, z_, z) for d, z_, _ in zs]
     for copy in agd_sent:
         copy.start()
-    for i in range(1, slabs // 2):
-        forward(ours + i, 0)
-
-    @pl.when(jnp.logical_not(edge))
-    def _():
-        spread_x()
 
     def core_sum(s):
         rsc(s).wait_recv()
@@ -653,13 +654,6 @@
     for i in range(1, slabs // 2):
         gate_terms = backward(theirs + i, gate_terms)
 
-    for d, _, zsrc in zs:
-        rsd(d, zsrc, zsrc).wait_recv()
-    total = rd[0].astype(F32)
-    for j in range(1, nz):
-        total = total + rd[j].astype(F32)
-    dsum[...] = total.astype(BF)
-    far_sum.start()
     agc(0, xl, xh, 1 - core).wait_recv()
     agc(3, xl, 1 - xh, 1 - core).wait_recv()
     cotangent(ours)
@@ -702,6 +696,14 @@
     for copy in arx_sent:
         copy.start()
     ax[xl * XH + xh, core] = pay[core, xh]
+
+    for d, _, zsrc in zs:
+        rsd(d, zsrc, zsrc).wait_recv()
+    total = rd[0].astype(F32)
+    for j in range(1, nz):
+        total = total + rd[j].astype(F32)
+    dsum[...] = total.astype(BF)
+    far_sum.start()
 
     for _, b in near:
         rsx2(b).wait_recv()

time: 54.9 us -> 53.5 us (0.974)
  Pallas kernels: 53.4 us -> 52 us
    pallas_call x1, Pallas kernels: 51.5 us -> 50.1 us  [body(): pl.pallas_call(functools.partial(kernel, nz, ny, hd, model, factor), out_...]
where the time goes in v5:
time: 53.5 us; the launch traced here: 53.3 us
  Pallas kernels  52 us (97%)
  between operations  1.29 us (2%)
    pallas_call x1, Pallas kernels, body(): pl.pallas_call(functools.partial(kernel, nz, ny, hd, model, factor), out_...  50.1 us
    pallas_call x1, Pallas kernels, body(): pl.pallas_call(hand_out, out_shape=out_shape, in_specs=[hbm] * 6, out_spe...  1.94 us

profile of v5, /device:TPU:1, one launch (start us, length us, event | category | flops | bytes accessed | tf_op | source)
XLA Modules:
  0.0 53.3 jit_solution(691780960745257453)
XLA Ops:
  1.3 50.1 %shard_map.163 = (bf16[1,16,16,512]{3,2,1,0:T(8,128)(2,1)}, bf16[1,16,16,512]{3,2,1,0:T(8,128)(2,1)}, bf16[1,16,16,512]{3,2,1,0:T(8,128)(2,1)}, f32[32,32]{1,0:T...) custom-call(bf16[1,16,16,512]{3,2,1,0:T(8,128)(2,1)} %q_in.1, bf16[1,16,16,512]{3,2,1,0:T(8,128)(2,1)} %k_in.1, ...), custom_call_target="tpu_custom_call" | custom-call | flops 2000000000 | bytes 4000000 | tf_op jit(solution)/shard_map/pallas_call | solution.py:880
  51.4 1.9 %shard_map.164 = (bf16[1,16,16,512]{3,2,1,0:T(8,128)(2,1)}, bf16[1,16,16,512]{3,2,1,0:T(8,128)(2,1)}, bf16[1,16,16,512]{3,2,1,0:T(8,128)(2,1)}, f32[32,32]{1,0:T...) custom-call(bf16[1,16,16,512]{3,2,1,0:T(8,128)(2,1)} %get-tuple-element.12.refs_0_, ...), custom_call_target="tpu_custom_call" | custom-call | tf_op jit(solution)/shard_map/pallas_call | solution.py:953
